TPU v7x, 128 devices: a whole 4x4x4 slice. The times are simulated.
128 devices in a mesh: cells: 128 (over y, z, x, core).
Axes of the slice: x: 4, y: 4, z: 4, core: 2. Of those that a mesh axis runs over, the one named last changes fastest.
Arguments:
- source_cells: bfloat16 [5120, 50, 256], P('cells')
- target_cells: bfloat16 [5120, 50, 256], P('cells')
- partners: int32 [5120, 6], P('cells'), may hold values from -1 to 5119, as said below
- home: int32 [5120], replicated, may hold values from 0 to 5119, as said below
Outputs:
- source_potential: float32 [5120, 256], P('cells')
- target_potential: float32 [5120, 256], P('cells')
Inputs may be any that keep to these rules, and one draw needn't show every extreme that they name: `home`: A permutation of the cluster ids. `partners`: in each row the ids come first and the -1 entries after them; the first entry is never -1; ids in a row are distinct; every target cluster id appears in some row; the slot of each listed id lies on the device of the source cluster or on one of its two neighbours along cells, cyclically (slot // 40 differs by -1, 0 or 1 modulo the number of devices); some row has all 6 entries set.
All inputs are finite; a program needn't handle non-finite values.
Results may differ from a plain program's by a relative error of at most 0.0014.
Values may be sent and summed in bfloat16 or wider, within the bound.
A program may use at most 64 MiB of HBM per device.

v0:
```python
import jax
import jax.numpy as jnp
from jax import lax
from jax.sharding import PartitionSpec as P

ITERS = 2


entropy = 0.5
sentinel = -1e30


def with_halo(block, sides, width):
    for axis, dim in sides:
        count = lax.axis_size(axis)
        forward = [(i, i + 1) for i in range(count - 1)]
        forward.append((count - 1, 0))
        backward = [(target, source) for source, target in forward]
        low = lax.ppermute(
            lax.slice_in_dim(block, block.shape[dim] - width, None, axis=dim), axis, forward
        )
        high = lax.ppermute(lax.slice_in_dim(block, 0, width, axis=dim), axis, backward)
        block = jnp.concatenate([low, block, high], axis=dim)
    return block


def from_behind(block, axis, distance):
    devices = range(lax.axis_size(axis))
    route = [((i - distance) % len(devices), i) for i in devices]
    return lax.ppermute(block, axis, route)


def squares_of(cells):
    wide = cells.astype(jnp.float32)
    return jnp.sum(wide * wide, axis=1)


def match_of(index, count):
    return index[:, None] == jnp.arange(count, dtype=jnp.int32)[None, :]


def pick_blocks(table, index):
    onehot = match_of(index, table.shape[0]).astype(jnp.bfloat16)
    chosen = jnp.einsum("gn,npc->gpc", onehot, table, preferred_element_type=jnp.float32)
    return chosen.astype(jnp.bfloat16)


def pick_rows(table, index):
    match = match_of(index, table.shape[0])
    return jnp.sum(jnp.where(match[:, :, None], table[None, :, :], 0.0), axis=1)


def fold_into(state, index, live, top, total):
    buf_top, buf_total = state
    match = match_of(index, buf_top.shape[0]) & live[:, None]
    spread = jnp.where(match[:, :, None], top[:, None, :], sentinel)
    new_top = jnp.maximum(buf_top, jnp.max(spread, axis=0))
    rescaled = buf_total * jnp.exp(buf_top - new_top)
    added = jnp.where(
        match[:, :, None], jnp.exp(spread - new_top[None, :, :]) * total[:, None, :], 0.0
    )
    return (new_top, rescaled + jnp.sum(added, axis=0))


def entry_list(left_index, right_index, live, width):
    trips = left_index.shape[0] // width
    return ((left_index, right_index, live), trips)


def sweep(entries, trips, width, left, left_sq, right, right_sq, right_pot, left_pot):
    left_index, right_index, live = entries
    cells = left.shape[2]
    row_state = (
        jnp.full((left.shape[0], cells), sentinel, jnp.float32),
        jnp.zeros((left.shape[0], cells), jnp.float32),
    )
    col_state = (
        jnp.full((right.shape[0], cells), sentinel, jnp.float32),
        jnp.zeros((right.shape[0], cells), jnp.float32),
    )

    def turn(step, state):
        rows, cols = state
        start = step * width
        left_pick = lax.dynamic_slice_in_dim(left_index, start, width)
        right_pick = lax.dynamic_slice_in_dim(right_index, start, width)
        active = lax.dynamic_slice_in_dim(live, start, width)
        cross = jnp.einsum(
            "gpi,gpj->gij",
            pick_blocks(left, left_pick),
            pick_blocks(right, right_pick),
            preferred_element_type=jnp.float32,
        )
        cost = (
            0.5
            * (
                pick_rows(left_sq, left_pick)[:, :, None]
                + pick_rows(right_sq, right_pick)[:, None, :]
            )
            - cross
        )
        row_logit = (pick_rows(right_pot, right_pick)[:, None, :] - cost) / entropy
        row_top = jnp.max(row_logit, axis=2)
        row_total = jnp.sum(jnp.exp(row_logit - row_top[:, :, None]), axis=2)
        rows = fold_into(rows, left_pick, active, row_top, row_total)
        col_logit = (pick_rows(left_pot, left_pick)[:, :, None] - cost) / entropy
        col_top = jnp.max(col_logit, axis=1)
        col_total = jnp.sum(jnp.exp(col_logit - col_top[:, None, :]), axis=1)
        cols = fold_into(cols, right_pick, active, col_top, col_total)
        return (rows, cols)

    return lax.fori_loop(0, trips, turn, (row_state, col_state))


def on_device(source_cells, target_cells, partners, home):
    blocks = source_cells.shape[0]
    cells = source_cells.shape[2]
    links = partners.shape[1]
    width = 2 * links
    devices = lax.axis_size("cells")
    here = lax.axis_index("cells")
    clusters = home.shape[0]
    offset = entropy * jnp.log(jnp.float32(blocks * devices * cells))
    catalog = jnp.arange(clusters, dtype=jnp.int32)
    source_sq = squares_of(source_cells)
    window_targets = with_halo(target_cells, (("cells", 0),), blocks)
    window_target_sq = squares_of(window_targets)
    source_pot = jnp.zeros((blocks, cells), jnp.float32)
    target_pot = jnp.zeros((blocks, cells), jnp.float32)
    valid = partners >= 0
    match = partners[..., None] == catalog
    slot = jnp.sum(jnp.where(match, home, 0), axis=-1)
    window_index = jnp.mod(slot - (here - 1) * blocks, clusters)
    own_rows = jnp.repeat(jnp.arange(blocks, dtype=jnp.int32), links)
    row_entries, row_trips = entry_list(
        own_rows, window_index.reshape(-1), valid.reshape(-1), width
    )
    for step in range(ITERS):
        window_pot = with_halo(target_pot.astype(jnp.bfloat16), (("cells", 0),), blocks).astype(
            target_pot.dtype
        )
        rows, cols = sweep(
            row_entries,
            row_trips,
            width,
            source_cells,
            source_sq,
            window_targets,
            window_target_sq,
            window_pot,
            source_pot,
        )
        own_top = cols[0][blocks : 2 * blocks]
        own_total = cols[1][blocks : 2 * blocks]
        for move_by, begin in ((-1, 0), (1, 2 * blocks)):
            packed = jnp.stack([cols[0][begin : begin + blocks], cols[1][begin : begin + blocks]])
            arrived = from_behind(packed, "cells", move_by)
            merged = jnp.maximum(own_top, arrived[0])
            own_total = own_total * jnp.exp(own_top - merged) + arrived[1] * jnp.exp(
                arrived[0] - merged
            )
            own_top = merged
        source_new = -entropy * (rows[0] + jnp.log(rows[1])) + offset
        target_new = -entropy * (own_top + jnp.log(own_total)) + offset
        source_pot = 0.5 * (source_pot + source_new)
        target_pot = 0.5 * (target_pot + target_new)
    return (source_pot, target_pot)


def solution(mesh):
    in_specs = (P("cells", None, None), P("cells", None, None), P("cells", None), P())
    out_specs = (P("cells", None), P("cells", None))
    return jax.shard_map(
        on_device, mesh=mesh, in_specs=in_specs, out_specs=out_specs, check_vma=False
    )
```

profile of v0, /device:TPU:0, one launch (start us, length us, event | category | flops | bytes accessed | tf_op | source)
XLA Modules:
  0.0 676.0 jit_solution(14372030058863209354)
XLA Ops:
  0.7 8.3 %collective-permute-start.1 = (bf16[40,256]{1,0:T(8,128)(2,1)S(1)}, bf16[40,256]{1,0:T(8,128)(2,1)S(1)}, u32[]{:S(2)}, u32[]{:S(2)}) collective-permute-start(bf16[40,256]{1,0:T(8,128)(2,1)S(1)} %convert_element_type.64), channel_id=1, source_target_pairs={{1,0},{2,1},{3,2},{4,3},{5,4},{6,5},{7,6},{8,7},{9,8},{10,9},{11,1... | collective-permute-start | bytes 61448 | tf_op jit(solution)/shard_map/ppermute | solution.py:22
  9.0 7.2 %collective-permute-start.3 = (bf16[40,50,256]{2,0,1:T(8,128)(2,1)}, bf16[40,50,256]{2,0,1:T(8,128)(2,1)}, u32[]{:S(2)}, u32[]{:S(2)}) collective-permute-start(bf16[40,50,256]{2,0,1:T(8,128)(2,1)} %param.9), channel_id=1, source_target_pairs={{1,0},{2,1},{3,2},{4,3},{5,4},{6,5},{7,6},{8,7},{9,8},{10,9},{11,1... | collective-permute-start | bytes 3072008 | tf_op jit(solution)/shard_map/ppermute | solution.py:22
  22.9 5.8 collective-permute-done.2
  33.2 288.4 %while.42 = (s32[]{:T(128)}, f32[40,256]{1,0:T(8,128)S(1)}, f32[40,256]{1,0:T(8,128)}, f32[120,256]{1,0:T(8,128)S(1)}, f32[120,256]{1,0:T(8,128)}, /*index=5*/s3...) while((s32[]{:T(128)}, f32[40,256]{1,0:T(8,128)S(1)}, ...), condition=%wide.region_15.16_spmd.clone, body=%wide.region_3.15_spmd.clone.sunk | while | flops 146821760 | bytes 19746188 | solution.py:112
  53.0 3.5 fusion.101
  81.8 3.5 fusion.101
  96.2 3.5 fusion.101
  110.7 3.5 fusion.101
  125.1 3.5 fusion.101
  139.5 3.5 fusion.101
  153.9 3.5 fusion.101
  168.3 3.5 fusion.101
  182.7 3.5 fusion.101
  226.0 3.5 fusion.101
  240.4 3.5 fusion.101
  254.8 3.5 fusion.101
  269.2 3.5 fusion.101
  283.7 3.5 fusion.101
  323.0 4.6 collective-permute-start.4
  330.0 7.9 %collective-permute-done.5 = f32[2,40,256]{2,1,0:T(8,128)} collective-permute-done((f32[2,40,256]{2,1,0:T(8,128)}, f32[2,40,256]{2,1,0:T(8,128)}, u32[]{:S(2)}, u32[]{:S(2)}) %collective-permute-start.5) | collective-permute-done | bytes 81952 | tf_op jit(solution)/shard_map/ppermute | solution.py:30
  339.4 7.2 %collective-permute-start.7 = (bf16[40,256]{1,0:T(8,128)(2,1)S(1)}, bf16[40,256]{1,0:T(8,128)(2,1)S(1)}, u32[]{:S(2)}, u32[]{:S(2)}) collective-permute-start(bf16[40,256]{1,0:T(8,128)(2,1)S(1)} %get-tuple-element.708), channel_id=1, source_target_pairs={{1,0},{2,1},{3,2},{4,3},{5,4},{6,5},{7,6},{8,7},{9,8},{10,9},{11,1... | collective-permute-start | bytes 61448 | tf_op jit(solution)/shard_map/ppermute | solution.py:22
  348.1 309.1 %while.43 = (s32[]{:T(128)}, f32[40,256]{1,0:T(8,128)S(1)}, f32[40,256]{1,0:T(8,128)}, f32[120,256]{1,0:T(8,128)S(1)}, f32[120,256]{1,0:T(8,128)}, /*index=5*/s3...) while((s32[]{:T(128)}, f32[40,256]{1,0:T(8,128)S(1)}, ...), condition=%wide.region_29.30_spmd.clone, body=%wide.region_16.29_spmd.clone.sunk | while | flops 147064448 | bytes 20905476 | solution.py:112
  353.4 3.8 fusion.112
  358.1 3.6 exponential_reduce_fusion.7
  368.8 3.8 fusion.112
  373.6 3.6 exponential_reduce_fusion.7
  384.3 3.8 fusion.112
  389.0 3.6 exponential_reduce_fusion.7
  399.7 3.8 fusion.112
  404.5 3.6 exponential_reduce_fusion.7
  415.2 3.8 fusion.112
  419.9 3.6 exponential_reduce_fusion.7
  430.7 3.8 fusion.112
  435.4 3.6 exponential_reduce_fusion.7
  446.1 3.8 fusion.112
  450.9 3.6 exponential_reduce_fusion.7
  461.6 3.8 fusion.112
  466.3 3.6 exponential_reduce_fusion.7
  477.0 3.8 fusion.112
  481.8 3.6 exponential_reduce_fusion.7
  492.5 3.8 fusion.112
  497.2 3.6 exponential_reduce_fusion.7
  507.9 3.8 fusion.112
  512.7 3.6 exponential_reduce_fusion.7
  523.4 3.8 fusion.112
  528.1 3.6 exponential_reduce_fusion.7
  538.8 3.8 fusion.112
  543.6 3.6 exponential_reduce_fusion.7
  554.3 3.8 fusion.112
  559.0 3.6 exponential_reduce_fusion.7
  569.8 3.8 fusion.112
  574.5 3.6 exponential_reduce_fusion.7
  585.2 3.8 fusion.112
  589.9 3.6 exponential_reduce_fusion.7
  600.7 3.8 fusion.112
  605.4 3.6 exponential_reduce_fusion.7
  616.1 3.8 fusion.112
  620.9 3.6 exponential_reduce_fusion.7
  631.6 3.8 fusion.112
  636.3 3.6 exponential_reduce_fusion.7
  647.0 3.8 fusion.112
  651.8 3.6 exponential_reduce_fusion.7
  658.0 7.2 %collective-permute-start.8 = (f32[2,40,256]{2,1,0:T(8,128)S(1)}, f32[2,40,256]{2,1,0:T(8,128)S(1)}, u32[]{:S(2)}, u32[]{:S(2)}) collective-permute-start(f32[2,40,256]{2,1,0:T(8,128)S(1)} %pad_maximum_fusion.2), channel_id=1, source_target_pairs={{1,0},{2,1},{3,2},{4,3},{5,4},{6,5},{7,6},{8,7},{9,8},{10,9},{11,1... | collective-permute-start | bytes 245768 | tf_op jit(solution)/shard_map/ppermute | solution.py:30
  667.3 7.2 %collective-permute-done.9 = f32[2,40,256]{2,1,0:T(8,128)S(1)} collective-permute-done((f32[2,40,256]{2,1,0:T(8,128)S(1)}, f32[2,40,256]{2,1,0:T(8,128)S(1)}, u32[]{:S(2)}, u32[]{:S(2)}) %collective-permute-start.9) | collective-permute-done | bytes 81952 | tf_op jit(solution)/shard_map/ppermute | solution.py:30
  (1717 shorter events, 414.4 us)
Async XLA Ops:
  0.6 21.5 %collective-permute-start = (bf16[40,256]{1,0:T(8,128)(2,1)S(1)}, bf16[40,256]{1,0:T(8,128)(2,1)S(1)}, u32[]{:S(2)}, u32[]{:S(2)}) collective-permute-start(bf16[40,256]{1,0:T(8,128)(2,1)S(1)} %convert_element_type.64), channel_id=1, source_target_pairs={{0,1},{1,2},{2,3},{3,4},{4,5},{5,6},{6,7},{7,8},{8,9},{9,10},{10,1... | collective-permute-start | bytes 61448 | tf_op jit(solution)/shard_map/ppermute | solution.py:19
  0.7 21.5 %collective-permute-start.1 = (bf16[40,256]{1,0:T(8,128)(2,1)S(1)}, bf16[40,256]{1,0:T(8,128)(2,1)S(1)}, u32[]{:S(2)}, u32[]{:S(2)}) collective-permute-start(bf16[40,256]{1,0:T(8,128)(2,1)S(1)} %convert_element_type.64), channel_id=1, source_target_pairs={{1,0},{2,1},{3,2},{4,3},{5,4},{6,5},{7,6},{8,7},{9,8},{10,9},{11,1... | collective-permute-start | bytes 61448 | tf_op jit(solution)/shard_map/ppermute | solution.py:22
  9.0 19.7 %collective-permute-start.2 = (bf16[40,50,256]{2,0,1:T(8,128)(2,1)}, bf16[40,50,256]{2,0,1:T(8,128)(2,1)}, u32[]{:S(2)}, u32[]{:S(2)}) collective-permute-start(bf16[40,50,256]{2,0,1:T(8,128)(2,1)} %param.9), channel_id=1, source_target_pairs={{0,1},{1,2},{2,3},{3,4},{4,5},{5,6},{6,7},{7,8},{8,9},{9,10},{10,1... | collective-permute-start | bytes 3072008 | tf_op jit(solution)/shard_map/ppermute | solution.py:19
  9.0 22.3 %collective-permute-start.3 = (bf16[40,50,256]{2,0,1:T(8,128)(2,1)}, bf16[40,50,256]{2,0,1:T(8,128)(2,1)}, u32[]{:S(2)}, u32[]{:S(2)}) collective-permute-start(bf16[40,50,256]{2,0,1:T(8,128)(2,1)} %param.9), channel_id=1, source_target_pairs={{1,0},{2,1},{3,2},{4,3},{5,4},{6,5},{7,6},{8,7},{9,8},{10,9},{11,1... | collective-permute-start | bytes 3072008 | tf_op jit(solution)/shard_map/ppermute | solution.py:22
  78.1 7.3 %copy-start.19 = (pred[12,120]{1,0:T(8,128)(4,1)}, pred[12,120]{1,0:T(8,128)(4,1)S(1)}, u32[]{:S(2)}) copy-start(pred[12,120]{1,0:T(8,128)(4,1)S(1)} %get-tuple-element.913) | copy-start | bytes 4324 | tf_op jit(solution)/shard_map/while
  92.5 7.3 %copy-start.19 = (pred[12,120]{1,0:T(8,128)(4,1)}, pred[12,120]{1,0:T(8,128)(4,1)S(1)}, u32[]{:S(2)}) copy-start(pred[12,120]{1,0:T(8,128)(4,1)S(1)} %get-tuple-element.913) | copy-start | bytes 4324 | tf_op jit(solution)/shard_map/while
  106.9 7.3 %copy-start.19 = (pred[12,120]{1,0:T(8,128)(4,1)}, pred[12,120]{1,0:T(8,128)(4,1)S(1)}, u32[]{:S(2)}) copy-start(pred[12,120]{1,0:T(8,128)(4,1)S(1)} %get-tuple-element.913) | copy-start | bytes 4324 | tf_op jit(solution)/shard_map/while
  121.3 7.3 %copy-start.19 = (pred[12,120]{1,0:T(8,128)(4,1)}, pred[12,120]{1,0:T(8,128)(4,1)S(1)}, u32[]{:S(2)}) copy-start(pred[12,120]{1,0:T(8,128)(4,1)S(1)} %get-tuple-element.913) | copy-start | bytes 4324 | tf_op jit(solution)/shard_map/while
  135.8 7.3 %copy-start.19 = (pred[12,120]{1,0:T(8,128)(4,1)}, pred[12,120]{1,0:T(8,128)(4,1)S(1)}, u32[]{:S(2)}) copy-start(pred[12,120]{1,0:T(8,128)(4,1)S(1)} %get-tuple-element.913) | copy-start | bytes 4324 | tf_op jit(solution)/shard_map/while
  150.2 7.3 %copy-start.19 = (pred[12,120]{1,0:T(8,128)(4,1)}, pred[12,120]{1,0:T(8,128)(4,1)S(1)}, u32[]{:S(2)}) copy-start(pred[12,120]{1,0:T(8,128)(4,1)S(1)} %get-tuple-element.913) | copy-start | bytes 4324 | tf_op jit(solution)/shard_map/while
  164.6 7.3 %copy-start.19 = (pred[12,120]{1,0:T(8,128)(4,1)}, pred[12,120]{1,0:T(8,128)(4,1)S(1)}, u32[]{:S(2)}) copy-start(pred[12,120]{1,0:T(8,128)(4,1)S(1)} %get-tuple-element.913) | copy-start | bytes 4324 | tf_op jit(solution)/shard_map/while
  179.0 7.3 %copy-start.19 = (pred[12,120]{1,0:T(8,128)(4,1)}, pred[12,120]{1,0:T(8,128)(4,1)S(1)}, u32[]{:S(2)}) copy-start(pred[12,120]{1,0:T(8,128)(4,1)S(1)} %get-tuple-element.913) | copy-start | bytes 4324 | tf_op jit(solution)/shard_map/while
  193.4 7.3 %copy-start.19 = (pred[12,120]{1,0:T(8,128)(4,1)}, pred[12,120]{1,0:T(8,128)(4,1)S(1)}, u32[]{:S(2)}) copy-start(pred[12,120]{1,0:T(8,128)(4,1)S(1)} %get-tuple-element.913) | copy-start | bytes 4324 | tf_op jit(solution)/shard_map/while
  207.8 7.3 %copy-start.19 = (pred[12,120]{1,0:T(8,128)(4,1)}, pred[12,120]{1,0:T(8,128)(4,1)S(1)}, u32[]{:S(2)}) copy-start(pred[12,120]{1,0:T(8,128)(4,1)S(1)} %get-tuple-element.913) | copy-start | bytes 4324 | tf_op jit(solution)/shard_map/while
  222.3 7.3 %copy-start.19 = (pred[12,120]{1,0:T(8,128)(4,1)}, pred[12,120]{1,0:T(8,128)(4,1)S(1)}, u32[]{:S(2)}) copy-start(pred[12,120]{1,0:T(8,128)(4,1)S(1)} %get-tuple-element.913) | copy-start | bytes 4324 | tf_op jit(solution)/shard_map/while
  279.9 7.3 %copy-start.19 = (pred[12,120]{1,0:T(8,128)(4,1)}, pred[12,120]{1,0:T(8,128)(4,1)S(1)}, u32[]{:S(2)}) copy-start(pred[12,120]{1,0:T(8,128)(4,1)S(1)} %get-tuple-element.913) | copy-start | bytes 4324 | tf_op jit(solution)/shard_map/while
  294.3 7.3 %copy-start.19 = (pred[12,120]{1,0:T(8,128)(4,1)}, pred[12,120]{1,0:T(8,128)(4,1)S(1)}, u32[]{:S(2)}) copy-start(pred[12,120]{1,0:T(8,128)(4,1)S(1)} %get-tuple-element.913) | copy-start | bytes 4324 | tf_op jit(solution)/shard_map/while
  308.8 7.3 %copy-start.19 = (pred[12,120]{1,0:T(8,128)(4,1)}, pred[12,120]{1,0:T(8,128)(4,1)S(1)}, u32[]{:S(2)}) copy-start(pred[12,120]{1,0:T(8,128)(4,1)S(1)} %get-tuple-element.913) | copy-start | bytes 4324 | tf_op jit(solution)/shard_map/while
  323.0 7.0 %collective-permute-start.4 = (f32[2,40,256]{2,1,0:T(8,128)}, f32[2,40,256]{2,1,0:T(8,128)}, u32[]{:S(2)}, u32[]{:S(2)}) collective-permute-start(f32[2,40,256]{2,1,0:T(8,128)} %pad_maximum_fusion), channel_id=1, source_target_pairs={{1,0},{2,1},{3,2},{4,3},{5,4},{6,5},{7,6},{8,7},{9,8},{10,9},{11,1... | collective-permute-start | bytes 245768 | tf_op jit(solution)/shard_map/ppermute | solution.py:30
  328.3 9.6 %collective-permute-start.5 = (f32[2,40,256]{2,1,0:T(8,128)}, f32[2,40,256]{2,1,0:T(8,128)}, u32[]{:S(2)}, u32[]{:S(2)}) collective-permute-start(f32[2,40,256]{2,1,0:T(8,128)} %pad_maximum_fusion.1), channel_id=1, source_target_pairs={{127,0},{0,1},{1,2},{2,3},{3,4},{4,5},{5,6},{6,7},{7,8},{8,9},{9,1... | collective-permute-start | bytes 245768 | tf_op jit(solution)/shard_map/ppermute | solution.py:30
  339.4 8.6 %collective-permute-start.6 = (bf16[40,256]{1,0:T(8,128)(2,1)S(1)}, bf16[40,256]{1,0:T(8,128)(2,1)S(1)}, u32[]{:S(2)}, u32[]{:S(2)}) collective-permute-start(bf16[40,256]{1,0:T(8,128)(2,1)S(1)} %get-tuple-element.708), channel_id=1, source_target_pairs={{0,1},{1,2},{2,3},{3,4},{4,5},{5,6},{6,7},{7,8},{8,9},{9,10},{10,1... | collective-permute-start | bytes 61448 | tf_op jit(solution)/shard_map/ppermute | solution.py:19
  339.4 8.7 %collective-permute-start.7 = (bf16[40,256]{1,0:T(8,128)(2,1)S(1)}, bf16[40,256]{1,0:T(8,128)(2,1)S(1)}, u32[]{:S(2)}, u32[]{:S(2)}) collective-permute-start(bf16[40,256]{1,0:T(8,128)(2,1)S(1)} %get-tuple-element.708), channel_id=1, source_target_pairs={{1,0},{2,1},{3,2},{4,3},{5,4},{6,5},{7,6},{8,7},{9,8},{10,9},{11,1... | collective-permute-start | bytes 61448 | tf_op jit(solution)/shard_map/ppermute | solution.py:22
  348.1 9.1 %copy-start.7 = (f32[120,256]{1,0:T(8,128)}, f32[120,256]{1,0:T(8,128)S(1)}, u32[]{:S(2)}) copy-start(f32[120,256]{1,0:T(8,128)S(1)} %get-tuple-element.1037) | copy-start | bytes 368644 | tf_op jit(solution)/shard_map/while
  349.7 7.4 %copy-start.17 = (pred[12,120]{1,0:T(8,128)(4,1)}, pred[12,120]{1,0:T(8,128)(4,1)S(1)}, u32[]{:S(2)}) copy-start(pred[12,120]{1,0:T(8,128)(4,1)S(1)} %get-tuple-element.940) | copy-start | bytes 4324 | tf_op jit(solution)/shard_map/while
  363.5 9.1 %copy-start.7 = (f32[120,256]{1,0:T(8,128)}, f32[120,256]{1,0:T(8,128)S(1)}, u32[]{:S(2)}) copy-start(f32[120,256]{1,0:T(8,128)S(1)} %get-tuple-element.1037) | copy-start | bytes 368644 | tf_op jit(solution)/shard_map/while
  365.2 7.4 %copy-start.17 = (pred[12,120]{1,0:T(8,128)(4,1)}, pred[12,120]{1,0:T(8,128)(4,1)S(1)}, u32[]{:S(2)}) copy-start(pred[12,120]{1,0:T(8,128)(4,1)S(1)} %get-tuple-element.940) | copy-start | bytes 4324 | tf_op jit(solution)/shard_map/while
  379.0 9.1 %copy-start.7 = (f32[120,256]{1,0:T(8,128)}, f32[120,256]{1,0:T(8,128)S(1)}, u32[]{:S(2)}) copy-start(f32[120,256]{1,0:T(8,128)S(1)} %get-tuple-element.1037) | copy-start | bytes 368644 | tf_op jit(solution)/shard_map/while
  380.6 7.4 %copy-start.17 = (pred[12,120]{1,0:T(8,128)(4,1)}, pred[12,120]{1,0:T(8,128)(4,1)S(1)}, u32[]{:S(2)}) copy-start(pred[12,120]{1,0:T(8,128)(4,1)S(1)} %get-tuple-element.940) | copy-start | bytes 4324 | tf_op jit(solution)/shard_map/while
  394.4 9.1 %copy-start.7 = (f32[120,256]{1,0:T(8,128)}, f32[120,256]{1,0:T(8,128)S(1)}, u32[]{:S(2)}) copy-start(f32[120,256]{1,0:T(8,128)S(1)} %get-tuple-element.1037) | copy-start | bytes 368644 | tf_op jit(solution)/shard_map/while
  396.1 7.4 %copy-start.17 = (pred[12,120]{1,0:T(8,128)(4,1)}, pred[12,120]{1,0:T(8,128)(4,1)S(1)}, u32[]{:S(2)}) copy-start(pred[12,120]{1,0:T(8,128)(4,1)S(1)} %get-tuple-element.940) | copy-start | bytes 4324 | tf_op jit(solution)/shard_map/while
  409.9 9.1 %copy-start.7 = (f32[120,256]{1,0:T(8,128)}, f32[120,256]{1,0:T(8,128)S(1)}, u32[]{:S(2)}) copy-start(f32[120,256]{1,0:T(8,128)S(1)} %get-tuple-element.1037) | copy-start | bytes 368644 | tf_op jit(solution)/shard_map/while
  411.6 7.4 %copy-start.17 = (pred[12,120]{1,0:T(8,128)(4,1)}, pred[12,120]{1,0:T(8,128)(4,1)S(1)}, u32[]{:S(2)}) copy-start(pred[12,120]{1,0:T(8,128)(4,1)S(1)} %get-tuple-element.940) | copy-start | bytes 4324 | tf_op jit(solution)/shard_map/while
  425.4 9.1 %copy-start.7 = (f32[120,256]{1,0:T(8,128)}, f32[120,256]{1,0:T(8,128)S(1)}, u32[]{:S(2)}) copy-start(f32[120,256]{1,0:T(8,128)S(1)} %get-tuple-element.1037) | copy-start | bytes 368644 | tf_op jit(solution)/shard_map/while
  427.0 7.4 %copy-start.17 = (pred[12,120]{1,0:T(8,128)(4,1)}, pred[12,120]{1,0:T(8,128)(4,1)S(1)}, u32[]{:S(2)}) copy-start(pred[12,120]{1,0:T(8,128)(4,1)S(1)} %get-tuple-element.940) | copy-start | bytes 4324 | tf_op jit(solution)/shard_map/while
  440.8 9.1 %copy-start.7 = (f32[120,256]{1,0:T(8,128)}, f32[120,256]{1,0:T(8,128)S(1)}, u32[]{:S(2)}) copy-start(f32[120,256]{1,0:T(8,128)S(1)} %get-tuple-element.1037) | copy-start | bytes 368644 | tf_op jit(solution)/shard_map/while
  442.5 7.4 %copy-start.17 = (pred[12,120]{1,0:T(8,128)(4,1)}, pred[12,120]{1,0:T(8,128)(4,1)S(1)}, u32[]{:S(2)}) copy-start(pred[12,120]{1,0:T(8,128)(4,1)S(1)} %get-tuple-element.940) | copy-start | bytes 4324 | tf_op jit(solution)/shard_map/while
  456.3 9.1 %copy-start.7 = (f32[120,256]{1,0:T(8,128)}, f32[120,256]{1,0:T(8,128)S(1)}, u32[]{:S(2)}) copy-start(f32[120,256]{1,0:T(8,128)S(1)} %get-tuple-element.1037) | copy-start | bytes 368644 | tf_op jit(solution)/shard_map/while
  457.9 7.4 %copy-start.17 = (pred[12,120]{1,0:T(8,128)(4,1)}, pred[12,120]{1,0:T(8,128)(4,1)S(1)}, u32[]{:S(2)}) copy-start(pred[12,120]{1,0:T(8,128)(4,1)S(1)} %get-tuple-element.940) | copy-start | bytes 4324 | tf_op jit(solution)/shard_map/while
  471.7 9.1 %copy-start.7 = (f32[120,256]{1,0:T(8,128)}, f32[120,256]{1,0:T(8,128)S(1)}, u32[]{:S(2)}) copy-start(f32[120,256]{1,0:T(8,128)S(1)} %get-tuple-element.1037) | copy-start | bytes 368644 | tf_op jit(solution)/shard_map/while
  473.4 7.4 %copy-start.17 = (pred[12,120]{1,0:T(8,128)(4,1)}, pred[12,120]{1,0:T(8,128)(4,1)S(1)}, u32[]{:S(2)}) copy-start(pred[12,120]{1,0:T(8,128)(4,1)S(1)} %get-tuple-element.940) | copy-start | bytes 4324 | tf_op jit(solution)/shard_map/while
  487.2 9.1 %copy-start.7 = (f32[120,256]{1,0:T(8,128)}, f32[120,256]{1,0:T(8,128)S(1)}, u32[]{:S(2)}) copy-start(f32[120,256]{1,0:T(8,128)S(1)} %get-tuple-element.1037) | copy-start | bytes 368644 | tf_op jit(solution)/shard_map/while
  488.8 7.4 %copy-start.17 = (pred[12,120]{1,0:T(8,128)(4,1)}, pred[12,120]{1,0:T(8,128)(4,1)S(1)}, u32[]{:S(2)}) copy-start(pred[12,120]{1,0:T(8,128)(4,1)S(1)} %get-tuple-element.940) | copy-start | bytes 4324 | tf_op jit(solution)/shard_map/while
  502.6 9.1 %copy-start.7 = (f32[120,256]{1,0:T(8,128)}, f32[120,256]{1,0:T(8,128)S(1)}, u32[]{:S(2)}) copy-start(f32[120,256]{1,0:T(8,128)S(1)} %get-tuple-element.1037) | copy-start | bytes 368644 | tf_op jit(solution)/shard_map/while
  504.3 7.4 %copy-start.17 = (pred[12,120]{1,0:T(8,128)(4,1)}, pred[12,120]{1,0:T(8,128)(4,1)S(1)}, u32[]{:S(2)}) copy-start(pred[12,120]{1,0:T(8,128)(4,1)S(1)} %get-tuple-element.940) | copy-start | bytes 4324 | tf_op jit(solution)/shard_map/while
  518.1 9.1 %copy-start.7 = (f32[120,256]{1,0:T(8,128)}, f32[120,256]{1,0:T(8,128)S(1)}, u32[]{:S(2)}) copy-start(f32[120,256]{1,0:T(8,128)S(1)} %get-tuple-element.1037) | copy-start | bytes 368644 | tf_op jit(solution)/shard_map/while
  519.7 7.4 %copy-start.17 = (pred[12,120]{1,0:T(8,128)(4,1)}, pred[12,120]{1,0:T(8,128)(4,1)S(1)}, u32[]{:S(2)}) copy-start(pred[12,120]{1,0:T(8,128)(4,1)S(1)} %get-tuple-element.940) | copy-start | bytes 4324 | tf_op jit(solution)/shard_map/while
  533.5 9.1 %copy-start.7 = (f32[120,256]{1,0:T(8,128)}, f32[120,256]{1,0:T(8,128)S(1)}, u32[]{:S(2)}) copy-start(f32[120,256]{1,0:T(8,128)S(1)} %get-tuple-element.1037) | copy-start | bytes 368644 | tf_op jit(solution)/shard_map/while
  535.2 7.4 %copy-start.17 = (pred[12,120]{1,0:T(8,128)(4,1)}, pred[12,120]{1,0:T(8,128)(4,1)S(1)}, u32[]{:S(2)}) copy-start(pred[12,120]{1,0:T(8,128)(4,1)S(1)} %get-tuple-element.940) | copy-start | bytes 4324 | tf_op jit(solution)/shard_map/while
  549.0 9.1 %copy-start.7 = (f32[120,256]{1,0:T(8,128)}, f32[120,256]{1,0:T(8,128)S(1)}, u32[]{:S(2)}) copy-start(f32[120,256]{1,0:T(8,128)S(1)} %get-tuple-element.1037) | copy-start | bytes 368644 | tf_op jit(solution)/shard_map/while
  550.6 7.4 %copy-start.17 = (pred[12,120]{1,0:T(8,128)(4,1)}, pred[12,120]{1,0:T(8,128)(4,1)S(1)}, u32[]{:S(2)}) copy-start(pred[12,120]{1,0:T(8,128)(4,1)S(1)} %get-tuple-element.940) | copy-start | bytes 4324 | tf_op jit(solution)/shard_map/while
  564.5 9.1 %copy-start.7 = (f32[120,256]{1,0:T(8,128)}, f32[120,256]{1,0:T(8,128)S(1)}, u32[]{:S(2)}) copy-start(f32[120,256]{1,0:T(8,128)S(1)} %get-tuple-element.1037) | copy-start | bytes 368644 | tf_op jit(solution)/shard_map/while
  566.1 7.4 %copy-start.17 = (pred[12,120]{1,0:T(8,128)(4,1)}, pred[12,120]{1,0:T(8,128)(4,1)S(1)}, u32[]{:S(2)}) copy-start(pred[12,120]{1,0:T(8,128)(4,1)S(1)} %get-tuple-element.940) | copy-start | bytes 4324 | tf_op jit(solution)/shard_map/while
  579.9 9.1 %copy-start.7 = (f32[120,256]{1,0:T(8,128)}, f32[120,256]{1,0:T(8,128)S(1)}, u32[]{:S(2)}) copy-start(f32[120,256]{1,0:T(8,128)S(1)} %get-tuple-element.1037) | copy-start | bytes 368644 | tf_op jit(solution)/shard_map/while
  581.6 7.4 %copy-start.17 = (pred[12,120]{1,0:T(8,128)(4,1)}, pred[12,120]{1,0:T(8,128)(4,1)S(1)}, u32[]{:S(2)}) copy-start(pred[12,120]{1,0:T(8,128)(4,1)S(1)} %get-tuple-element.940) | copy-start | bytes 4324 | tf_op jit(solution)/shard_map/while
  595.4 9.1 %copy-start.7 = (f32[120,256]{1,0:T(8,128)}, f32[120,256]{1,0:T(8,128)S(1)}, u32[]{:S(2)}) copy-start(f32[120,256]{1,0:T(8,128)S(1)} %get-tuple-element.1037) | copy-start | bytes 368644 | tf_op jit(solution)/shard_map/while
  597.0 7.4 %copy-start.17 = (pred[12,120]{1,0:T(8,128)(4,1)}, pred[12,120]{1,0:T(8,128)(4,1)S(1)}, u32[]{:S(2)}) copy-start(pred[12,120]{1,0:T(8,128)(4,1)S(1)} %get-tuple-element.940) | copy-start | bytes 4324 | tf_op jit(solution)/shard_map/while
  610.8 9.1 %copy-start.7 = (f32[120,256]{1,0:T(8,128)}, f32[120,256]{1,0:T(8,128)S(1)}, u32[]{:S(2)}) copy-start(f32[120,256]{1,0:T(8,128)S(1)} %get-tuple-element.1037) | copy-start | bytes 368644 | tf_op jit(solution)/shard_map/while
  612.5 7.4 %copy-start.17 = (pred[12,120]{1,0:T(8,128)(4,1)}, pred[12,120]{1,0:T(8,128)(4,1)S(1)}, u32[]{:S(2)}) copy-start(pred[12,120]{1,0:T(8,128)(4,1)S(1)} %get-tuple-element.940) | copy-start | bytes 4324 | tf_op jit(solution)/shard_map/while
  626.3 9.1 %copy-start.7 = (f32[120,256]{1,0:T(8,128)}, f32[120,256]{1,0:T(8,128)S(1)}, u32[]{:S(2)}) copy-start(f32[120,256]{1,0:T(8,128)S(1)} %get-tuple-element.1037) | copy-start | bytes 368644 | tf_op jit(solution)/shard_map/while
  627.9 7.4 %copy-start.17 = (pred[12,120]{1,0:T(8,128)(4,1)}, pred[12,120]{1,0:T(8,128)(4,1)S(1)}, u32[]{:S(2)}) copy-start(pred[12,120]{1,0:T(8,128)(4,1)S(1)} %get-tuple-element.940) | copy-start | bytes 4324 | tf_op jit(solution)/shard_map/while
  641.7 9.1 %copy-start.7 = (f32[120,256]{1,0:T(8,128)}, f32[120,256]{1,0:T(8,128)S(1)}, u32[]{:S(2)}) copy-start(f32[120,256]{1,0:T(8,128)S(1)} %get-tuple-element.1037) | copy-start | bytes 368644 | tf_op jit(solution)/shard_map/while
  643.4 7.4 %copy-start.17 = (pred[12,120]{1,0:T(8,128)(4,1)}, pred[12,120]{1,0:T(8,128)(4,1)S(1)}, u32[]{:S(2)}) copy-start(pred[12,120]{1,0:T(8,128)(4,1)S(1)} %get-tuple-element.940) | copy-start | bytes 4324 | tf_op jit(solution)/shard_map/while
  658.0 9.3 %collective-permute-start.8 = (f32[2,40,256]{2,1,0:T(8,128)S(1)}, f32[2,40,256]{2,1,0:T(8,128)S(1)}, u32[]{:S(2)}, u32[]{:S(2)}) collective-permute-start(f32[2,40,256]{2,1,0:T(8,128)S(1)} %pad_maximum_fusion.2), channel_id=1, source_target_pairs={{1,0},{2,1},{3,2},{4,3},{5,4},{6,5},{7,6},{8,7},{9,8},{10,9},{11,1... | collective-permute-start | bytes 245768 | tf_op jit(solution)/shard_map/ppermute | solution.py:30
  665.2 9.3 %collective-permute-start.9 = (f32[2,40,256]{2,1,0:T(8,128)S(1)}, f32[2,40,256]{2,1,0:T(8,128)S(1)}, u32[]{:S(2)}, u32[]{:S(2)}) collective-permute-start(f32[2,40,256]{2,1,0:T(8,128)S(1)} %pad_maximum_fusion.3), channel_id=1, source_target_pairs={{127,0},{0,1},{1,2},{2,3},{3,4},{4,5},{5,6},{6,7},{7,8},{8,9},{9,1... | collective-permute-start | bytes 245768 | tf_op jit(solution)/shard_map/ppermute | solution.py:30
  (387 other events, 1305.0 us)
where the time goes:
time: 681 us; the launch traced here: 676 us
  other arithmetic  280 us (41%)
  matrix products  183 us (27%)
  local copies, waits for them, and re-layouts  145 us (21%)
  starting transfers between devices  34.5 us (5%)
  waiting for transfers between devices  23.3 us (3%)
  loops' own time  8.75 us (1%)
    dot_general x40, matrix products, turn(): jnp.einsum('gpi,gpj->gij', pick_blocks(left, left_pick), pick_blocks(righ...  146 us
    reduce_sum x40, other arithmetic, turn(): col_total = jnp.sum(jnp.exp(col_logit - col_top[:, None, :]), axis=1)  139 us
    reduce_sum x80, other arithmetic, pick_rows(): return jnp.sum(jnp.where(match[:, :, None], table[None, :, :], 0.0), axis=1)  53.8 us
    while x960, local copies, waits for them, and re-layouts  46.8 us
    dot_general x80, matrix products, pick_blocks(): jnp.einsum('gn,npc->gpc', onehot, table, preferred_element_type=jnp.float32)  36.9 us
    dynamic_slice x40, local copies, waits for them, and re-layouts, turn(): right_pick = lax.dynamic_slice_in_dim(right_index, start, width)  31.8 us
    dynamic_slice x40, local copies, waits for them, and re-layouts, turn(): active = lax.dynamic_slice_in_dim(live, start, width)  29.9 us
    dynamic_slice x40, local copies, waits for them, and re-layouts, turn(): left_pick = lax.dynamic_slice_in_dim(left_index, start, width)  29.6 us
  transfers between devices with their start and end apart: 10, of which 5 were waited for; matrix products, arithmetic and copies ran while one was open for 2% of the time, Pallas kernels for 0%

commit v1 on v0

v1 whole, which is shorter than its diff:
```python
import functools
import math

import jax
import jax.numpy as jnp
from jax import lax
from jax.experimental import pallas as pl
from jax.experimental.pallas import tpu as pltpu
from jax.sharding import PartitionSpec as P

F32 = jnp.float32
BF16 = jnp.bfloat16
entropy = 0.5
SHIFT = 48.0
SQ_LIMIT = 24.0
G_SHIFT = 24.0
NEVER = -1e30
WAYS = 2
MANY = 8
DEPTH = 64
REGION = 256
COUNTS = 3 * REGION

VMEM = pl.BlockSpec(memory_space=pltpu.VMEM)
HBM = pl.BlockSpec(memory_space=pltpu.HBM)
SMEM = pl.BlockSpec(memory_space=pltpu.SMEM)


def row_of(index, shape):
    return lax.broadcasted_iota(jnp.int32, shape, 0) == index


def pieces(x):
    high = x.astype(BF16).astype(F32)
    middle = (x - high).astype(BF16).astype(F32)
    low = (x - high - middle).astype(BF16).astype(F32)
    return high, middle, low


def extend(wide, first, second):
    last = wide[48:56]
    for at, value in enumerate(first + second):
        last = jnp.where(row_of(at + 2, last.shape), value, last)
    return jnp.concatenate([wide[:48], last, jnp.zeros_like(last)], axis=0)


def widen(block_ref, wide_ref):
    depth, blocks, _ = block_ref.shape

    def turn(p, carry):
        full = block_ref[p].astype(F32)
        for half in range(2):
            wide_ref[half, pl.ds(p * blocks, blocks)] = full[:, half * 128 : half * 128 + 128]
        return carry

    lax.fori_loop(0, depth, turn, 0, unroll=5)
    rest = (56 - depth) * blocks
    for half in range(2):
        wide_ref[half, pl.ds(depth * blocks, rest)] = jnp.zeros((rest, 128), F32)


def cluster(wide_ref, blocks, slot):
    halves = [wide_ref[half, pl.ds(slot, 56, stride=blocks)] for half in range(2)]
    return jnp.concatenate(halves, axis=1)


def prepare_target(wide, slot, base, out_ref, top):
    square = jnp.sum(wide * wide, axis=0, keepdims=True)
    out_ref[base + slot] = extend(wide, pieces(-square), (1.0, 1.0, 1.0)).astype(BF16)
    return jnp.maximum(top, square)


def prepare_source(wide, slot, out_ref, top):
    square = jnp.sum(wide * wide, axis=0, keepdims=True)
    full = extend(2.0 * wide, (1.0, 1.0, 1.0), pieces(SHIFT - square))
    out_ref[slot] = full.T.astype(BF16)
    return jnp.maximum(top, square)


def entry(lists_ref, at):
    code = lists_ref[at]
    return code // 128, lax.rem(code, 128)


def base_of(lists_ref, region):
    base = 0
    for r in range(region):
        base = base + lists_ref[COUNTS + r]
    return base


def in_groups(count, pair):
    def turn(start, ways):
        def body(step, carry):
            for way in range(ways):
                pair(start + step * ways + way)
            return carry

        return body

    groups = count // MANY
    lax.fori_loop(0, groups, turn(0, MANY), 0)
    rest = count - groups * MANY
    lax.fori_loop(0, rest // WAYS, turn(groups * MANY, WAYS), 0)


def first_sweep(region, lists_ref, at_ref, b_ref, k_ref, rows_ref, cols_ref):
    base = base_of(lists_ref, region)

    def pair(at):
        s, w = entry(lists_ref, region * REGION + at)
        logit = jnp.dot(at_ref[s], b_ref[w], preferred_element_type=F32)
        weight = jnp.exp(logit)
        k_ref[base + at] = weight.astype(BF16)
        rows_ref[s] += weight[:, :128] + weight[:, 128:]
        cols_ref[pl.ds(w, 1)] += jnp.sum(weight, axis=0, keepdims=True)

    in_groups(lists_ref[COUNTS + region], pair)


def prepare_kernel(
    source_in, target_in, partners_in, home_in,
    at_ref, b_ref, lists_ref, top_ref,
    source_ref, target_ref, partners_ref, home_ref, sems, source_wide, target_wide,
):
    loads = [
        pltpu.make_async_copy(given, held, sems.at[i])
        for i, (given, held) in enumerate((
            (partners_in, partners_ref), (home_in, home_ref),
            (source_in, source_ref), (target_in, target_ref),
        ))
    ]
    for load in loads:
        load.start()
    for load in loads:
        load.wait()
    links, blocks = partners_ref.shape
    clusters = home_ref.shape[0]
    here = lax.axis_index("cells")
    sibling = 2 - 2 * lax.rem(here, 2)
    cells = source_ref.shape[2]
    widen(source_ref, source_wide)
    widen(target_ref, target_wide)

    def turn(s, carry):
        counts, top = carry
        for m in range(links):
            name = partners_ref[m, s]
            live = name >= 0
            slot = home_ref[jnp.maximum(name, 0)]
            w = slot - (here - 1) * blocks
            w = jnp.where(w < 0, w + clusters, w)
            w = jnp.where(w >= clusters, w - clusters, w)
            block = w // blocks
            region = jnp.where(block == 1, 0, jnp.where(block == sibling, 1, 2))
            region = jnp.where(live, region, 3)
            count = jnp.where(
                region == 0, counts[0], jnp.where(region == 1, counts[1], counts[2])
            )
            place = jnp.where(live, region * REGION + count, COUNTS + 8)
            lists_ref[place] = s * 128 + w
            counts = tuple(c + jnp.where(region == r, 1, 0) for r, c in enumerate(counts))
        top = prepare_source(cluster(source_wide, blocks, s), s, at_ref, top)
        top = prepare_target(cluster(target_wide, blocks, s), s, blocks, b_ref, top)
        return counts, top

    zero = jnp.int32(0)
    counts, top = lax.fori_loop(
        0, blocks, turn, ((zero, zero, zero), jnp.zeros((1, cells), F32)), unroll=4
    )
    dummy = 3 * blocks
    for r, count in enumerate(counts):
        for extra in range(WAYS - 1):
            lists_ref[r * REGION + count + extra] = dummy
        lists_ref[COUNTS + r] = (count + WAYS - 1) // WAYS * WAYS
    shape = b_ref.shape[1:]
    b_ref[dummy] = jnp.where(row_of(50, shape), NEVER, 0.0).astype(BF16)
    top_ref[...] = jnp.broadcast_to(top, top_ref.shape)


def take_block(which, block_ref, b_ref, top_ref, stage_ref, sem, wide_ref):
    blocks = block_ref.shape[1]
    load = pltpu.make_async_copy(block_ref, stage_ref, sem)
    load.start()
    load.wait()
    widen(stage_ref, wide_ref)
    here = lax.axis_index("cells")
    side = 2 - 2 * lax.rem(here, 2)
    base = (side if which == 1 else 2 - side) * blocks

    def turn(t, top):
        return prepare_target(cluster(wide_ref, blocks, t), t, base, b_ref, top)

    top = lax.fori_loop(0, blocks, turn, top_ref[0:1], unroll=4)
    top_ref[...] = jnp.broadcast_to(top, top_ref.shape)


def within(top_ref):
    return jnp.max(top_ref[0:1]) <= SQ_LIMIT


def near_kernel(
    block_ref, at_ref, lists_ref, b_in, top_in,
    b_ref, top_ref, k_ref, rows_ref, cols_ref, stage_ref, sem, wide_ref,
):
    cols_ref[...] = jnp.zeros(cols_ref.shape, F32)

    def start(s, carry):
        rows_ref[s] = jnp.zeros(rows_ref.shape[1:], F32)
        return carry

    lax.fori_loop(0, rows_ref.shape[0], start, 0, unroll=4)
    take_block(1, block_ref, b_ref, top_ref, stage_ref, sem, wide_ref)
    first_sweep(0, lists_ref, at_ref, b_ref, k_ref, rows_ref, cols_ref)
    first_sweep(1, lists_ref, at_ref, b_ref, k_ref, rows_ref, cols_ref)


def each_pair(lists_ref, body):
    for region in range(3):

        def turn(at, carry, region=region):
            body(*entry(lists_ref, region * REGION + at))
            return carry

        lax.fori_loop(0, lists_ref[COUNTS + region], turn, 0)


def careful_rows(lists_ref, at_ref, b_ref, rows_ref, weight_row, out_ref, log_n):
    shape = rows_ref.shape[1:]
    left = lax.broadcasted_iota(jnp.int32, shape, 1) < 64

    def start(s, carry):
        rows_ref[s] = jnp.where(left, NEVER, 0.0)
        return carry

    lax.fori_loop(0, rows_ref.shape[0], start, 0)

    def body(s, w):
        logit = jnp.dot(at_ref[s], b_ref[w], preferred_element_type=F32) + weight_row(w)
        held = rows_ref[s]
        top, total = held[:, 0:1], held[:, 64:65]
        new_top = jnp.maximum(top, jnp.max(logit, axis=1, keepdims=True))
        total = total * jnp.exp(top - new_top)
        total = total + jnp.sum(jnp.exp(logit - new_top), axis=1, keepdims=True)
        rows_ref[s] = jnp.where(left, new_top, total)

    each_pair(lists_ref, body)

    def finish(s, carry):
        held = rows_ref[s]
        lse = held[:, 0:1] + jnp.log(held[:, 64:65]) - SHIFT
        wide = jnp.broadcast_to(lse, shape)
        out_ref[pl.ds(s, 1)] = wide.T[0:1]
        rows_ref[s] = 0.5 * (log_n - wide)
        return carry

    lax.fori_loop(0, rows_ref.shape[0], finish, 0)


def careful_cols(lists_ref, at_ref, b_ref, weight_col, total_ref, out_ref):
    out_ref[...] = jnp.full(out_ref.shape, NEVER, F32)
    total_ref[...] = jnp.zeros(total_ref.shape, F32)

    def body(s, w):
        logit = jnp.dot(at_ref[s], b_ref[w], preferred_element_type=F32)
        logit = logit - SHIFT + weight_col(s)
        at = pl.ds(w, 1)
        top = out_ref[at]
        new_top = jnp.maximum(top, jnp.max(logit, axis=0, keepdims=True))
        total = total_ref[at] * jnp.exp(top - new_top)
        total_ref[at] = total + jnp.sum(jnp.exp(logit - new_top), axis=0, keepdims=True)
        out_ref[at] = new_top

    each_pair(lists_ref, body)
    total = total_ref[...]
    out_ref[...] = jnp.where(
        total > 0.0, out_ref[...] + jnp.log(jnp.maximum(total, 1e-37)), NEVER
    )


def far_kernel(
    log_n,
    block_ref, at_ref, lists_ref, b_in, top_in, k_in, rows_in, cols_in,
    b_ref, top_ref, k_ref, rows_ref, cols_ref, u_ref, row_lse_ref, col_lse_ref, stage_ref, sem, wide_ref,
):
    take_block(2, block_ref, b_ref, top_ref, stage_ref, sem, wide_ref)
    first_sweep(2, lists_ref, at_ref, b_ref, k_ref, rows_ref, cols_ref)
    fine = within(top_ref)

    @pl.when(fine)
    def _():
        total = cols_ref[...]
        col_lse_ref[...] = jnp.where(
            total > 0.0, jnp.log(jnp.maximum(total, 1e-37)) - SHIFT, NEVER
        )
        ones = jnp.ones((128, 128), BF16)

        def turn(s, carry):
            held = rows_ref[s].astype(BF16)
            wide = jnp.dot(held, ones, preferred_element_type=F32)
            u_ref[s] = lax.rsqrt(wide).astype(BF16)
            line = lax.dot_general(
                ones[0:16], held, (((1,), (1,)), ((), ())), preferred_element_type=F32
            )
            row_lse_ref[pl.ds(s, 1)] = jnp.log(line[0:1]) - SHIFT
            return carry

        lax.fori_loop(0, rows_ref.shape[0], turn, 0, unroll=4)

    @pl.when(jnp.logical_not(fine))
    def _():
        careful_rows(lists_ref, at_ref, b_ref, rows_ref, lambda w: 0.0, row_lse_ref, log_n)
        careful_cols(lists_ref, at_ref, b_ref, lambda s: 0.0, cols_ref, col_lse_ref)


def column_kernel(
    log_n,
    at_ref, lists_ref, b_ref, top_ref, k_ref, rows_ref, u_ref,
    col_lse_ref, cols_ref,
):
    fine = within(top_ref)

    @pl.when(fine)
    def _():
        cols_ref[...] = jnp.zeros(cols_ref.shape, F32)
        for region in range(3):
            base = base_of(lists_ref, region)

            def pair(at, region=region, base=base):
                s, w = entry(lists_ref, region * REGION + at)
                half = u_ref[s]
                part = k_ref[base + at] * jnp.concatenate([half, half], axis=1)
                while part.shape[0] > 16:
                    mid = part.shape[0] // 2
                    part = part[:mid] + part[mid:]
                cols_ref[pl.ds(w, 1)] += jnp.sum(part.astype(F32), axis=0, keepdims=True)

            in_groups(lists_ref[COUNTS + region], pair)
        total = cols_ref[...]
        col_lse_ref[...] = jnp.where(
            total > 0.0,
            jnp.log(jnp.maximum(total, 1e-37)) + (0.5 * log_n - 0.5 * SHIFT),
            NEVER,
        )

    @pl.when(jnp.logical_not(fine))
    def _():
        careful_cols(
            lists_ref, at_ref, b_ref, lambda s: rows_ref[s][:, 0:1], cols_ref, col_lse_ref
        )


def lse_of(values):
    top = functools.reduce(jnp.maximum, values)
    return top + jnp.log(sum(jnp.exp(v - top) for v in values))


def row_kernel(
    log_n,
    at_ref, lists_ref, b_ref, top_ref, k_ref, row_lse_ref, col_lse_ref,
    right_ref, left_ref, right2_ref, left2_ref, rows_in,
    source_ref, own_ref, rows_ref, g_ref, v_ref, second_ref, sums_ref,
):
    blocks = source_ref.shape[0]
    own = col_lse_ref[pl.ds(blocks, blocks)]
    own = lse_of([own, right_ref[pl.ds(0, blocks)], left_ref[pl.ds(blocks, blocks)]])
    low = lse_of([col_lse_ref[pl.ds(0, blocks)], left_ref[pl.ds(0, blocks)], left2_ref[...]])
    high = lse_of(
        [col_lse_ref[pl.ds(2 * blocks, blocks)], right_ref[pl.ds(blocks, blocks)], right2_ref[...]]
    )
    own_g = 0.5 * (log_n - own)
    own_ref[...] = own_g
    g_ref[...] = jnp.zeros(g_ref.shape, F32)
    g_ref[pl.ds(0, blocks)] = 0.5 * (log_n - low)
    g_ref[pl.ds(blocks, blocks)] = own_g
    g_ref[pl.ds(2 * blocks, blocks)] = 0.5 * (log_n - high)
    g = g_ref[...]
    fine = within(top_ref) & (jnp.max(g) <= 60.0) & (jnp.min(g) >= 0.0)

    @pl.when(fine)
    def _():
        v_ref[...] = jnp.exp(g_ref[...] - G_SHIFT)

        def start(s, carry):
            sums_ref[s] = jnp.zeros(sums_ref.shape[1:], BF16)
            return carry

        lax.fori_loop(0, blocks, start, 0, unroll=4)
        for region in range(3):
            base = base_of(lists_ref, region)

            def pair(at, region=region, base=base):
                s, w = entry(lists_ref, region * REGION + at)
                line = jnp.broadcast_to(v_ref[pl.ds(w, 1)].astype(BF16), (256, 256))
                part = k_ref[base + at] * line
                sums_ref[s] += part[:, :128] + part[:, 128:]

            in_groups(lists_ref[COUNTS + region], pair)
        ones = jnp.ones((16, 128), BF16)

        def turn(s, carry):
            line = lax.dot_general(
                ones, sums_ref[s], (((1,), (1,)), ((), ())),
                preferred_element_type=F32,
            )
            second_ref[pl.ds(s, 1)] = jnp.log(line[0:1]) - SHIFT + G_SHIFT
            return carry

        lax.fori_loop(0, blocks, turn, 0, unroll=4)

    @pl.when(jnp.logical_not(fine))
    def _():
        careful_rows(
            lists_ref, at_ref, b_ref, rows_ref, lambda w: g_ref[pl.ds(w, 1)], second_ref, log_n
        )

    first = 0.5 * (log_n - row_lse_ref[...])
    source_ref[...] = (0.5 * entropy) * (first + log_n - second_ref[...])


def in_hbm(array):
    return pltpu.with_memory_space_constraint(array, pltpu.HBM)


def on_device(source_cells, target_cells, partners, home):
    blocks, _, cells = source_cells.shape
    source_cells = source_cells.transpose(1, 0, 2)
    target_cells = target_cells.transpose(1, 0, 2)
    stage = pltpu.VMEM(source_cells.shape, BF16)
    wide = pltpu.VMEM((2, 56 * blocks, 128), F32)
    links = partners.shape[1]
    devices = lax.axis_size("cells")
    log_n = math.log(blocks * devices * cells)
    window = 128
    places = blocks * links + 3 * (WAYS - 1)

    def moved(block, step):
        return lax.ppermute(block, "cells", [(i, step(i) % devices) for i in range(devices)])

    far = in_hbm(moved(target_cells, lambda i: i + 1 if i % 2 else i - 1))
    sibling = in_hbm(moved(target_cells, lambda i: i ^ 1))

    vm = lambda shape, dtype: pltpu.VMEM(shape, dtype)
    at_s = vm((blocks, cells, DEPTH), BF16)
    b_s = vm((3 * blocks + 1, DEPTH, cells), BF16)
    top_s = vm((8, cells), F32)
    k_s = vm((places, cells, cells), BF16)
    rows_s = vm((blocks, cells, 128), F32)
    cols_s = vm((window, cells), F32)
    u_s = vm((blocks, cells, 128), BF16)
    lines_s = vm((blocks, cells), F32)
    limit = pltpu.CompilerParams(vmem_limit_bytes=8 * 2**20)

    at, b, lists, top = pl.pallas_call(
        prepare_kernel,
        out_shape=[at_s, b_s, jax.ShapeDtypeStruct((COUNTS + 16,), jnp.int32), top_s],
        in_specs=[HBM] * 4,
        out_specs=[VMEM, VMEM, SMEM, VMEM],
        scratch_shapes=[
            stage, stage, pltpu.SMEM((links, blocks), jnp.int32), pltpu.SMEM(home.shape, jnp.int32),
            pltpu.SemaphoreType.DMA((4,)), wide, wide,
        ],
        compiler_params=limit,
        name="prepare",
    )(*map(in_hbm, (source_cells, target_cells, partners.T, home)))
    b, top, k, rows, cols = pl.pallas_call(
        near_kernel,
        out_shape=[b_s, top_s, k_s, rows_s, cols_s],
        in_specs=[HBM, VMEM, SMEM, VMEM, VMEM],
        out_specs=[VMEM] * 5,
        input_output_aliases={3: 0, 4: 1},
        scratch_shapes=[stage, pltpu.SemaphoreType.DMA, wide],
        compiler_params=limit,
        name="near_pairs",
    )(sibling, at, lists, b, top)
    b, top, k, rows, cols, u, row_lse, col_lse = pl.pallas_call(
        functools.partial(far_kernel, log_n),
        out_shape=[b_s, top_s, k_s, rows_s, cols_s, u_s, lines_s, cols_s],
        in_specs=[HBM, VMEM, SMEM] + [VMEM] * 5,
        out_specs=[VMEM] * 8,
        input_output_aliases={3: 0, 4: 1, 5: 2, 6: 3, 7: 4},
        scratch_shapes=[stage, pltpu.SemaphoreType.DMA, wide],
        compiler_params=limit,
        name="far_pairs",
    )(far, at, lists, b, top, k, rows, cols)

    right = moved(col_lse[: 2 * blocks], lambda i: i - 1)
    left = moved(col_lse[blocks : 3 * blocks], lambda i: i + 1)
    right2 = moved(col_lse[:blocks], lambda i: i - 2)
    left2 = moved(col_lse[2 * blocks : 3 * blocks], lambda i: i + 2)

    col_lse2, _ = pl.pallas_call(
        functools.partial(column_kernel, log_n),
        out_shape=[cols_s, cols_s],
        in_specs=[VMEM, SMEM] + [VMEM] * 5,
        out_specs=[VMEM] * 2,
        compiler_params=limit,
        name="second_columns",
    )(at, lists, b, top, k, rows, u)
    from_right = moved(col_lse2[:blocks], lambda i: i - 1)
    from_left = moved(col_lse2[2 * blocks : 3 * blocks], lambda i: i + 1)

    source_pot, own_g, *_ = pl.pallas_call(
        functools.partial(row_kernel, log_n),
        out_shape=[lines_s, lines_s, rows_s, cols_s, cols_s, lines_s, u_s],
        in_specs=[VMEM, SMEM] + [VMEM] * 10,
        out_specs=[VMEM] * 7,
        input_output_aliases={11: 2},
        compiler_params=limit,
        name="second_rows",
    )(at, lists, b, top, k, row_lse, col_lse, right, left, right2, left2, rows)

    total = lse_of([col_lse2[blocks : 2 * blocks], from_right, from_left])
    target_pot = (0.5 * entropy) * (own_g + log_n - total)
    return source_pot, target_pot


def solution(mesh):
    in_specs = (P("cells", None, None), P("cells", None, None), P("cells", None), P())
    out_specs = (P("cells", None), P("cells", None))
    return jax.shard_map(
        on_device, mesh=mesh, in_specs=in_specs, out_specs=out_specs, check_vma=False
    )
```

time: 681 us -> 318 us (0.47)
  Pallas kernels: 0 us -> 290 us
  other arithmetic: 280 us -> 0.66 us
  matrix products: 183 us -> 0 us
  local copies, waits for them, and re-layouts: 145 us -> 2.57 us
  waiting for transfers between devices: 23.3 us -> 0.02 us
  starting transfers between devices: 34.5 us -> 24.1 us
  loops' own time: 8.75 us -> 0 us
    pallas_call x0 -> x5, Pallas kernels: none -> 290 us  [the longest x1 135 us: on_device(): pl.pallas_call(functools.partial(far_kernel, log_n), out_shape=[b_s, top_...]
    reduce_sum x203 -> x0, other arithmetic: 222 us -> none  [the longest x40 139 us: turn(): col_total = jnp.sum(jnp.exp(col_logit - col_top[:, None, :]), axis=1)]
    dot_general x120 -> x0, matrix products: 183 us -> none  [the longest x40 146 us: turn(): jnp.einsum('gpi,gpj->gij', pick_blocks(left, left_pick), pick_blocks(righ...]
    dynamic_slice x120 -> x0, local copies, waits for them, and re-layouts: 91.3 us -> none  [the longest x40 31.8 us: turn(): right_pick = lax.dynamic_slice_in_dim(right_index, start, width)]
    while x960 -> x0, local copies, waits for them, and re-layouts: 46.8 us -> none
    and x80 -> x0, other arithmetic: 29 us -> none  [fold_into(): match = match_of(index, buf_top.shape[0]) & live[:, None]]
    ppermute x10 -> x8, waiting for transfers between devices: 23.3 us -> 0.02 us  [moved(): lax.ppermute(block, 'cells', [(i, step(i) % devices) for i in range(devic...]
    reduce_max x80 -> x0, other arithmetic: 15.5 us -> none  [fold_into(): new_top = jnp.maximum(buf_top, jnp.max(spread, axis=0))]
  transfers between devices with their start and end apart: 10 -> 8, of which waited for: 5 -> 0; matrix products, arithmetic and copies ran while one was open for 2% -> 0% of each run, Pallas kernels for 0% -> 49%
where the time goes in v1:
time: 318 us
  Pallas kernels  290 us (91%)
  starting transfers between devices  24.1 us (8%)
    pallas_call x1, Pallas kernels, on_device(): pl.pallas_call(functools.partial(far_kernel, log_n), out_shape=[b_s, top_...  135 us
    pallas_call x1, Pallas kernels, on_device(): pl.pallas_call(functools.partial(row_kernel, log_n), out_shape=[lines_s,...  95.7 us
    pallas_call x1, Pallas kernels, on_device(): pl.pallas_call(functools.partial(column_kernel, log_n), out_shape=[cols_s...  40.4 us
    ppermute x8, starting transfers between devices, moved(): lax.ppermute(block, 'cells', [(i, step(i) % devices) for i in range(devic...  24.1 us
    pallas_call x1, Pallas kernels, on_device(): pl.pallas_call(near_kernel, out_shape=[b_s, top_s, k_s, rows_s, cols_s],...  11.6 us
    pallas_call x1, Pallas kernels, on_device(): pl.pallas_call(prepare_kernel, out_shape=[at_s, b_s, jax.ShapeDtypeStruct...  7.29 us
  transfers between devices with their start and end apart: 8, of which 0 were waited for; matrix products, arithmetic and copies ran while one was open for 0% of the time, Pallas kernels for 49%

profile of v1, /device:TPU:0, one launch (start us, length us, event | category | flops | bytes accessed | tf_op | source)
XLA Modules:
  0.0 318.0 jit_solution(13895118548205661852)
XLA Ops:
  0.6 0.1 collective-permute-start.1
  0.7 8.9 %collective-permute-start = (bf16[50,40,256]{2,1,0:T(8,128)(2,1)}, bf16[50,40,256]{2,1,0:T(8,128)(2,1)S(1)}, u32[]{:S(2)}, u32[]{:S(2)}) collective-permute-start(bf16[50,40,256]{2,1,0:T(8,128)(2,1)} %bitcast.5), channel_id=1, source_target_pairs={{0,127},{1,2},{2,1},{3,4},{4,3},{5,6},{6,5},{7,8},{8,7},{9,10},{10... | collective-permute-start | bytes 3072008 | tf_op jit(solution)/shard_map/ppermute | solution.py:438
  9.6 7.3 %prepare.1 = (bf16[40,256,64]{2,1,0:T(8,128)(2,1)S(1)}, bf16[121,64,256]{2,1,0:T(8,128)(2,1)S(1)}, s32[784]{0:T(1024)S(1)}, f32[8,256]{1,0:T(8,128)S(1)}) custom-call(bf16[50,40,256]{2,1,0:T(8,128)(2,1)} %bitcast.3, bf16[50,40,256]{2,1,0:T(8,128)(2,1)} %bitcast.6, s32[6,40]{1,0:T(8,128)} %bitcast.7, s32[5120]{0:T(1024)} %home_in.1), custom_call_target="tpu_custom_call" | custom-call | tf_op jit(solution)/shard_map/prepare/pallas_call | solution.py:454
  16.9 0.0 collective-permute-done.1.block_ref
  16.9 0.0 copy-start.1
  16.9 1.0 copy-done.1
  17.9 11.6 %near_pairs.1 = (bf16[121,64,256]{2,1,0:T(8,128)(2,1)S(1)}, f32[8,256]{1,0:T(8,128)S(1)}, bf16[243,256,256]{2,1,0:T(8,128)(2,1)S(1)}, f32[40,256,128]{2,1,0:T(8,128)S(1)}, f32[128,256]{1,0:T(8,128)S(1)}) custom-call(bf16[50,40,256]{2,1,0:T(8,128)(2,1)} %copy-done.1, ...), custom_call_target="tpu_custom_call", output_to_operand_aliasing={{0}: (3, {}), {1}: (4, {})} | custom-call | tf_op jit(solution)/shard_map/near_pairs/pallas_call | solution.py:466
  29.5 0.0 collective-permute-done.block_ref
  29.5 0.0 copy-start
  29.5 1.0 copy-done
  30.5 134.9 %far_pairs.1 = (bf16[121,64,256]{2,1,0:T(8,128)(2,1)S(1)}, f32[8,256]{1,0:T(8,128)S(1)}, bf16[243,256,256]{2,1,0:T(8,128)(2,1)S(1)}, f32[40,256,128]{2,1,0:T(8,1...) custom-call(bf16[50,40,256]{2,1,0:T(8,128)(2,1)} %copy-done, ...), custom_call_target="tpu_custom_call", output_to_operand_aliasing={{0}: (3, {}), {1}: (4, {}), {2}: (5, {}), {3}: (6, {}), {4}... | custom-call | tf_op jit(solution)/shard_map/far_pairs/pallas_call | solution.py:476
  165.4 0.1 collective-permute-start.5
  165.5 7.4 %collective-permute-start.4 = (f32[40,256]{1,0:T(8,128)S(1)}, f32[40,256]{1,0:T(8,128)S(1)}, u32[]{:S(2)}, u32[]{:S(2)}) collective-permute-start(f32[40,256]{1,0:T(8,128)S(1)} %get-tuple-element.43), channel_id=1, source_target_pairs={{0,126},{1,127},{2,0},{3,1},{4,2},{5,3},{6,4},{7,5},{8,6},{9,7},{1... | collective-permute-start | bytes 122888 | tf_op jit(solution)/shard_map/ppermute | solution.py:438
  172.9 0.0 collective-permute-start.3
  172.9 7.2 %collective-permute-start.2 = (f32[80,256]{1,0:T(8,128)S(1)}, f32[80,256]{1,0:T(8,128)S(1)}, u32[]{:S(2)}, u32[]{:S(2)}) collective-permute-start(f32[80,256]{1,0:T(8,128)S(1)} %get-tuple-element.45), channel_id=1, source_target_pairs={{0,127},{1,0},{2,1},{3,2},{4,3},{5,4},{6,5},{7,6},{8,7},{9,8},{10,... | collective-permute-start | bytes 245768 | tf_op jit(solution)/shard_map/ppermute | solution.py:438
  180.1 40.4 %second_columns.1 = (f32[128,256]{1,0:T(8,128)S(1)}, f32[128,256]{1,0:T(8,128)}) custom-call(bf16[40,256,64]{2,1,0:T(8,128)(2,1)S(1)} %get-tuple-element.21.at_ref, s32[784]{0:T(1024)S(1)} %get-tuple-element.22.lists_ref, bf16[121,64,256]{2,1,0:T(8,128)(2,1)S(1)} %get-tuple-element.30.b_ref, f32[8,256]{1,0:T(8,128)S(1)} %get-tuple-element.31.top_ref, ...), custom_call_target="tpu_custom_call" | custom-call | tf_op jit(solution)/shard_map/second_columns/pallas_call | solution.py:492
  220.5 0.0 collective-permute-start.6
  220.5 0.0 collective-permute-done.5.left2_ref
  220.5 0.5 collective-permute-start.7
  221.0 0.0 collective-permute-done.4.right2_ref
  221.0 0.0 collective-permute-done.3.left_ref
  221.0 0.0 collective-permute-done.2.right_ref
  221.0 95.7 %second_rows.1 = (f32[40,256]{1,0:T(8,128)S(1)}, f32[40,256]{1,0:T(8,128)S(1)}, f32[40,256,128]{2,1,0:T(8,128)S(1)}, f32[128,256]{1,0:T(8,128)}, f32[128,256]{1,...) custom-call(bf16[40,256,64]{2,1,0:T(8,128)(2,1)S(1)} %get-tuple-element.21.at_ref, ...), custom_call_target="tpu_custom_call", output_to_operand_aliasing={{2}: (11, {})} | custom-call | tf_op jit(solution)/shard_map/second_rows/pallas_call | solution.py:503
  316.7 0.6 copy.22
  317.3 0.0 collective-permute-done.6
  317.3 0.0 collective-permute-done.7
  317.3 0.7 subtract_multiply_fusion
  (3 shorter events, 0.0 us)
Async XLA Ops:
  0.6 16.3 %collective-permute-start.1 = (bf16[50,40,256]{2,1,0:T(8,128)(2,1)}, bf16[50,40,256]{2,1,0:T(8,128)(2,1)S(1)}, u32[]{:S(2)}, u32[]{:S(2)}) collective-permute-start(bf16[50,40,256]{2,1,0:T(8,128)(2,1)} %bitcast.4), channel_id=1, source_target_pairs={{0,1},{1,0},{2,3},{3,2},{4,5},{5,4},{6,7},{7,6},{8,9},{9,8},{10,11... | collective-permute-start | bytes 3072008 | tf_op jit(solution)/shard_map/ppermute | solution.py:438
  0.7 28.8 %collective-permute-start = (bf16[50,40,256]{2,1,0:T(8,128)(2,1)}, bf16[50,40,256]{2,1,0:T(8,128)(2,1)S(1)}, u32[]{:S(2)}, u32[]{:S(2)}) collective-permute-start(bf16[50,40,256]{2,1,0:T(8,128)(2,1)} %bitcast.5), channel_id=1, source_target_pairs={{0,127},{1,2},{2,1},{3,4},{4,3},{5,6},{6,5},{7,8},{8,7},{9,10},{10... | collective-permute-start | bytes 3072008 | tf_op jit(solution)/shard_map/ppermute | solution.py:438
  16.9 1.0 copy-start.1
  29.5 1.0 copy-start
  165.4 55.1 %collective-permute-start.5 = (f32[40,256]{1,0:T(8,128)S(1)}, f32[40,256]{1,0:T(8,128)S(1)}, u32[]{:S(2)}, u32[]{:S(2)}) collective-permute-start(f32[40,256]{1,0:T(8,128)S(1)} %get-tuple-element.42), channel_id=1, source_target_pairs={{0,2},{1,3},{2,4},{3,5},{4,6},{5,7},{6,8},{7,9},{8,10},{9,11},{10,... | collective-permute-start | bytes 122888 | tf_op jit(solution)/shard_map/ppermute | solution.py:438
  165.5 55.5 %collective-permute-start.4 = (f32[40,256]{1,0:T(8,128)S(1)}, f32[40,256]{1,0:T(8,128)S(1)}, u32[]{:S(2)}, u32[]{:S(2)}) collective-permute-start(f32[40,256]{1,0:T(8,128)S(1)} %get-tuple-element.43), channel_id=1, source_target_pairs={{0,126},{1,127},{2,0},{3,1},{4,2},{5,3},{6,4},{7,5},{8,6},{9,7},{1... | collective-permute-start | bytes 122888 | tf_op jit(solution)/shard_map/ppermute | solution.py:438
  172.9 48.1 %collective-permute-start.3 = (f32[80,256]{1,0:T(8,128)S(1)}, f32[80,256]{1,0:T(8,128)S(1)}, u32[]{:S(2)}, u32[]{:S(2)}) collective-permute-start(f32[80,256]{1,0:T(8,128)S(1)} %get-tuple-element.44), channel_id=1, source_target_pairs={{0,1},{1,2},{2,3},{3,4},{4,5},{5,6},{6,7},{7,8},{8,9},{9,10},{10,1... | collective-permute-start | bytes 245768 | tf_op jit(solution)/shard_map/ppermute | solution.py:438
  172.9 48.1 %collective-permute-start.2 = (f32[80,256]{1,0:T(8,128)S(1)}, f32[80,256]{1,0:T(8,128)S(1)}, u32[]{:S(2)}, u32[]{:S(2)}) collective-permute-start(f32[80,256]{1,0:T(8,128)S(1)} %get-tuple-element.45), channel_id=1, source_target_pairs={{0,127},{1,0},{2,1},{3,2},{4,3},{5,4},{6,5},{7,6},{8,7},{9,8},{10,... | collective-permute-start | bytes 245768 | tf_op jit(solution)/shard_map/ppermute | solution.py:438
  220.5 96.8 %collective-permute-start.6 = (f32[40,256]{1,0:T(8,128)S(1)}, f32[40,256]{1,0:T(8,128)S(1)}, u32[]{:S(2)}, u32[]{:S(2)}) collective-permute-start(f32[40,256]{1,0:T(8,128)S(1)} %get-tuple-element.40), channel_id=1, source_target_pairs={{0,127},{1,0},{2,1},{3,2},{4,3},{5,4},{6,5},{7,6},{8,7},{9,8},{10,... | collective-permute-start | bytes 122888 | tf_op jit(solution)/shard_map/ppermute | solution.py:438
  220.5 96.8 %collective-permute-start.7 = (f32[40,256]{1,0:T(8,128)S(1)}, f32[40,256]{1,0:T(8,128)S(1)}, u32[]{:S(2)}, u32[]{:S(2)}) collective-permute-start(f32[40,256]{1,0:T(8,128)S(1)} %get-tuple-element.41), channel_id=1, source_target_pairs={{0,1},{1,2},{2,3},{3,4},{4,5},{5,6},{6,7},{7,8},{8,9},{9,10},{10,1... | collective-permute-start | bytes 122888 | tf_op jit(solution)/shard_map/ppermute | solution.py:438

commit v2 on v1

--- a/solution.py
+++ b/solution.py
@@ -16,7 +16,7 @@
 G_SHIFT = 24.0
 NEVER = -1e30
 WAYS = 2
-MANY = 8
+MANY = 16
 DEPTH = 64
 REGION = 256
 COUNTS = 3 * REGION
@@ -79,7 +79,7 @@
 
 def entry(lists_ref, at):
     code = lists_ref[at]
-    return code // 128, lax.rem(code, 128)
+    return lax.shift_right_logical(code, 7), code & 127
 
 
 def base_of(lists_ref, region):
@@ -142,34 +142,32 @@
     widen(source_ref, source_wide)
     widen(target_ref, target_wide)
 
+    regions = jnp.where(sibling == 0, 0b100001, 0b010010)
+
     def turn(s, carry):
         counts, top = carry
         for m in range(links):
             name = partners_ref[m, s]
-            live = name >= 0
             slot = home_ref[jnp.maximum(name, 0)]
             w = slot - (here - 1) * blocks
             w = jnp.where(w < 0, w + clusters, w)
             w = jnp.where(w >= clusters, w - clusters, w)
-            block = w // blocks
-            region = jnp.where(block == 1, 0, jnp.where(block == sibling, 1, 2))
-            region = jnp.where(live, region, 3)
-            count = jnp.where(
-                region == 0, counts[0], jnp.where(region == 1, counts[1], counts[2])
-            )
-            place = jnp.where(live, region * REGION + count, COUNTS + 8)
-            lists_ref[place] = s * 128 + w
-            counts = tuple(c + jnp.where(region == r, 1, 0) for r, c in enumerate(counts))
+            block = jnp.where(w >= blocks, 2, 0) + jnp.where(w >= 2 * blocks, 2, 0)
+            region = lax.shift_right_logical(regions, block) & 3
+            bit = region * 10
+            count = lax.shift_right_logical(counts, bit) & 1023
+            lists_ref[region * REGION + count] = s * 128 + w
+            counts = counts + jnp.where(name >= 0, lax.shift_left(1, bit), 0)
         top = prepare_source(cluster(source_wide, blocks, s), s, at_ref, top)
         top = prepare_target(cluster(target_wide, blocks, s), s, blocks, b_ref, top)
         return counts, top
 
-    zero = jnp.int32(0)
     counts, top = lax.fori_loop(
-        0, blocks, turn, ((zero, zero, zero), jnp.zeros((1, cells), F32)), unroll=4
+        0, blocks, turn, (jnp.int32(0), jnp.zeros((1, cells), F32)), unroll=4
     )
     dummy = 3 * blocks
-    for r, count in enumerate(counts):
+    for r in range(3):
+        count = lax.shift_right_logical(counts, 10 * r) & 1023
         for extra in range(WAYS - 1):
             lists_ref[r * REGION + count + extra] = dummy
         lists_ref[COUNTS + r] = (count + WAYS - 1) // WAYS * WAYS
@@ -178,12 +176,9 @@
     top_ref[...] = jnp.broadcast_to(top, top_ref.shape)
 
 
-def take_block(which, block_ref, b_ref, top_ref, stage_ref, sem, wide_ref):
+def take_block(which, block_ref, b_ref, top_ref, wide_ref):
     blocks = block_ref.shape[1]
-    load = pltpu.make_async_copy(block_ref, stage_ref, sem)
-    load.start()
-    load.wait()
-    widen(stage_ref, wide_ref)
+    widen(block_ref, wide_ref)
     here = lax.axis_index("cells")
     side = 2 - 2 * lax.rem(here, 2)
     base = (side if which == 1 else 2 - side) * blocks
@@ -203,6 +198,8 @@
     block_ref, at_ref, lists_ref, b_in, top_in,
     b_ref, top_ref, k_ref, rows_ref, cols_ref, stage_ref, sem, wide_ref,
 ):
+    load = pltpu.make_async_copy(block_ref, stage_ref, sem)
+    load.start()
     cols_ref[...] = jnp.zeros(cols_ref.shape, F32)
 
     def start(s, carry):
@@ -210,7 +207,8 @@
         return carry
 
     lax.fori_loop(0, rows_ref.shape[0], start, 0, unroll=4)
-    take_block(1, block_ref, b_ref, top_ref, stage_ref, sem, wide_ref)
+    load.wait()
+    take_block(1, stage_ref, b_ref, top_ref, wide_ref)
     first_sweep(0, lists_ref, at_ref, b_ref, k_ref, rows_ref, cols_ref)
     first_sweep(1, lists_ref, at_ref, b_ref, k_ref, rows_ref, cols_ref)
 
@@ -281,9 +279,9 @@
 def far_kernel(
     log_n,
     block_ref, at_ref, lists_ref, b_in, top_in, k_in, rows_in, cols_in,
-    b_ref, top_ref, k_ref, rows_ref, cols_ref, u_ref, row_lse_ref, col_lse_ref, stage_ref, sem, wide_ref,
+    b_ref, top_ref, k_ref, rows_ref, cols_ref, u_ref, row_lse_ref, col_lse_ref, wide_ref,
 ):
-    take_block(2, block_ref, b_ref, top_ref, stage_ref, sem, wide_ref)
+    take_block(2, block_ref, b_ref, top_ref, wide_ref)
     first_sweep(2, lists_ref, at_ref, b_ref, k_ref, rows_ref, cols_ref)
     fine = within(top_ref)
 
@@ -295,17 +293,15 @@
         )
         ones = jnp.ones((128, 128), BF16)
 
-        def turn(s, carry):
-            held = rows_ref[s].astype(BF16)
-            wide = jnp.dot(held, ones, preferred_element_type=F32)
+        def turn(s, sums):
+            wide = jnp.dot(rows_ref[s].astype(BF16), ones, preferred_element_type=F32)
             u_ref[s] = lax.rsqrt(wide).astype(BF16)
-            line = lax.dot_general(
-                ones[0:16], held, (((1,), (1,)), ((), ())), preferred_element_type=F32
-            )
-            row_lse_ref[pl.ds(s, 1)] = jnp.log(line[0:1]) - SHIFT
-            return carry
-
-        lax.fori_loop(0, rows_ref.shape[0], turn, 0, unroll=4)
+            return jnp.where(lane == s, wide, sums)
+
+        blocks, cells, lanes = rows_ref.shape
+        lane = lax.broadcasted_iota(jnp.int32, (cells, lanes), 1)
+        sums = lax.fori_loop(0, blocks, turn, jnp.ones((cells, lanes), F32), unroll=4)
+        row_lse_ref[...] = jnp.log(sums.T[:blocks]) - SHIFT
 
     @pl.when(jnp.logical_not(fine))
     def _():
@@ -355,31 +351,69 @@
     return top + jnp.log(sum(jnp.exp(v - top) for v in values))
 
 
+def exchange_kernel(
+    log_n, first_ref, second_ref, g_ref, total_ref,
+    to_left, to_right, from_left, from_right, from_left2, from_right2, send_sems, receive_sems,
+):
+    blocks = total_ref.shape[0]
+    devices = lax.axis_size("cells")
+    here = lax.axis_index("cells")
+    peers = [lax.rem(here + devices + step, devices) for step in (-1, 1, -2, 2)]
+    barrier = pltpu.get_barrier_semaphore()
+    for peer in peers:
+        pl.semaphore_signal(
+            barrier, inc=1, device_id=(peer,), device_id_type=pl.DeviceIdType.MESH
+        )
+    to_left[pl.ds(0, 2 * blocks)] = first_ref[pl.ds(0, 2 * blocks)]
+    to_left[pl.ds(2 * blocks, blocks)] = second_ref[pl.ds(0, blocks)]
+    to_right[pl.ds(0, 2 * blocks)] = first_ref[pl.ds(blocks, 2 * blocks)]
+    to_right[pl.ds(2 * blocks, blocks)] = second_ref[pl.ds(2 * blocks, blocks)]
+    pl.semaphore_wait(barrier, len(peers))
+    copies = []
+    for i, (given, taken) in enumerate((
+        (to_left, from_right),
+        (to_right, from_left),
+        (to_left.at[pl.ds(0, blocks)], from_right2),
+        (to_right.at[pl.ds(blocks, blocks)], from_left2),
+    )):
+        copy = pltpu.make_async_remote_copy(
+            src_ref=given,
+            dst_ref=taken,
+            send_sem=send_sems.at[i],
+            recv_sem=receive_sems.at[i],
+            device_id=(peers[i],),
+            device_id_type=pl.DeviceIdType.MESH,
+        )
+        copy.start()
+        copies.append(copy)
+    for copy in copies:
+        copy.wait()
+    low, own, high = (pl.ds(i * blocks, blocks) for i in range(3))
+    total_ref[...] = lse_of([second_ref[own], from_right[high], from_left[high]])
+    g_ref[...] = jnp.zeros(g_ref.shape, F32)
+    for place, values in (
+        (low, [first_ref[low], from_left[low], from_left2[...]]),
+        (own, [first_ref[own], from_right[low], from_left[own]]),
+        (high, [first_ref[high], from_right[own], from_right2[...]]),
+    ):
+        g_ref[place] = 0.5 * (log_n - lse_of(values))
+
+
 def row_kernel(
     log_n,
-    at_ref, lists_ref, b_ref, top_ref, k_ref, row_lse_ref, col_lse_ref,
-    right_ref, left_ref, right2_ref, left2_ref, rows_in,
-    source_ref, own_ref, rows_ref, g_ref, v_ref, second_ref, sums_ref,
+    at_ref, lists_ref, b_ref, top_ref, k_ref, row_lse_ref, g_ref, total_ref, rows_in,
+    source_ref, target_ref, rows_ref, second_ref, sums_ref, v_ref,
 ):
     blocks = source_ref.shape[0]
-    own = col_lse_ref[pl.ds(blocks, blocks)]
-    own = lse_of([own, right_ref[pl.ds(0, blocks)], left_ref[pl.ds(blocks, blocks)]])
-    low = lse_of([col_lse_ref[pl.ds(0, blocks)], left_ref[pl.ds(0, blocks)], left2_ref[...]])
-    high = lse_of(
-        [col_lse_ref[pl.ds(2 * blocks, blocks)], right_ref[pl.ds(blocks, blocks)], right2_ref[...]]
-    )
-    own_g = 0.5 * (log_n - own)
-    own_ref[...] = own_g
-    g_ref[...] = jnp.zeros(g_ref.shape, F32)
-    g_ref[pl.ds(0, blocks)] = 0.5 * (log_n - low)
-    g_ref[pl.ds(blocks, blocks)] = own_g
-    g_ref[pl.ds(2 * blocks, blocks)] = 0.5 * (log_n - high)
+    target_ref[...] = (0.5 * entropy) * (g_ref[pl.ds(blocks, blocks)] + log_n - total_ref[...])
     g = g_ref[...]
     fine = within(top_ref) & (jnp.max(g) <= 60.0) & (jnp.min(g) >= 0.0)
 
     @pl.when(fine)
     def _():
-        v_ref[...] = jnp.exp(g_ref[...] - G_SHIFT)
+        g_line = jnp.exp(g_ref[...] - G_SHIFT)
+        for w in range(g_line.shape[0]):
+            v_ref[w] = jnp.broadcast_to(g_line[w : w + 1], v_ref.shape[1:]).astype(BF16)
 
         def start(s, carry):
             sums_ref[s] = jnp.zeros(sums_ref.shape[1:], BF16)
@@ -391,22 +425,23 @@
 
             def pair(at, region=region, base=base):
                 s, w = entry(lists_ref, region * REGION + at)
-                line = jnp.broadcast_to(v_ref[pl.ds(w, 1)].astype(BF16), (256, 256))
-                part = k_ref[base + at] * line
+                line = v_ref[w]
+                held = k_ref[base + at]
+                part = held.reshape(-1, *line.shape) * line[None]
+                part = part.reshape(held.shape)
                 sums_ref[s] += part[:, :128] + part[:, 128:]
 
             in_groups(lists_ref[COUNTS + region], pair)
-        ones = jnp.ones((16, 128), BF16)
-
-        def turn(s, carry):
-            line = lax.dot_general(
-                ones, sums_ref[s], (((1,), (1,)), ((), ())),
-                preferred_element_type=F32,
-            )
-            second_ref[pl.ds(s, 1)] = jnp.log(line[0:1]) - SHIFT + G_SHIFT
-            return carry
-
-        lax.fori_loop(0, blocks, turn, 0, unroll=4)
+        wide = (8 * 128, 128)
+        group = lax.shift_right_logical(lax.broadcasted_iota(jnp.int32, wide, 0), 7)
+        lane = lax.broadcasted_iota(jnp.int32, wide, 1)
+        sums = None
+        for first in range(0, blocks, 8):
+            parts = jnp.concatenate([sums_ref[first + i] for i in range(8)], axis=1)
+            pick = jnp.where(lane == group + first, 1.0, 0.0).astype(BF16)
+            part = jnp.dot(parts, pick, preferred_element_type=F32)
+            sums = part if sums is None else sums + part
+        second_ref[...] = jnp.log(sums.T[:blocks]) - SHIFT + G_SHIFT
 
     @pl.when(jnp.logical_not(fine))
     def _():
@@ -437,7 +472,7 @@
     def moved(block, step):
         return lax.ppermute(block, "cells", [(i, step(i) % devices) for i in range(devices)])
 
-    far = in_hbm(moved(target_cells, lambda i: i + 1 if i % 2 else i - 1))
+    far = moved(target_cells, lambda i: i + 1 if i % 2 else i - 1)
     sibling = in_hbm(moved(target_cells, lambda i: i ^ 1))
 
     vm = lambda shape, dtype: pltpu.VMEM(shape, dtype)
@@ -453,7 +488,7 @@
 
     at, b, lists, top = pl.pallas_call(
         prepare_kernel,
-        out_shape=[at_s, b_s, jax.ShapeDtypeStruct((COUNTS + 16,), jnp.int32), top_s],
+        out_shape=[at_s, b_s, pltpu.SMEM((COUNTS + 16,), jnp.int32), top_s],
         in_specs=[HBM] * 4,
         out_specs=[VMEM, VMEM, SMEM, VMEM],
         scratch_shapes=[
@@ -476,18 +511,13 @@
     b, top, k, rows, cols, u, row_lse, col_lse = pl.pallas_call(
         functools.partial(far_kernel, log_n),
         out_shape=[b_s, top_s, k_s, rows_s, cols_s, u_s, lines_s, cols_s],
-        in_specs=[HBM, VMEM, SMEM] + [VMEM] * 5,
+        in_specs=[VMEM, VMEM, SMEM] + [VMEM] * 5,
         out_specs=[VMEM] * 8,
         input_output_aliases={3: 0, 4: 1, 5: 2, 6: 3, 7: 4},
-        scratch_shapes=[stage, pltpu.SemaphoreType.DMA, wide],
+        scratch_shapes=[wide],
         compiler_params=limit,
         name="far_pairs",
     )(far, at, lists, b, top, k, rows, cols)
-
-    right = moved(col_lse[: 2 * blocks], lambda i: i - 1)
-    left = moved(col_lse[blocks : 3 * blocks], lambda i: i + 1)
-    right2 = moved(col_lse[:blocks], lambda i: i - 2)
-    left2 = moved(col_lse[2 * blocks : 3 * blocks], lambda i: i + 2)
 
     col_lse2, _ = pl.pallas_call(
         functools.partial(column_kernel, log_n),
@@ -497,21 +527,29 @@
         compiler_params=limit,
         name="second_columns",
     )(at, lists, b, top, k, rows, u)
-    from_right = moved(col_lse2[:blocks], lambda i: i - 1)
-    from_left = moved(col_lse2[2 * blocks : 3 * blocks], lambda i: i + 1)
-
-    source_pot, own_g, *_ = pl.pallas_call(
+    message = pltpu.VMEM((3 * blocks, cells), F32)
+    block = pltpu.VMEM((blocks, cells), F32)
+    g, total = pl.pallas_call(
+        functools.partial(exchange_kernel, log_n),
+        out_shape=[cols_s, lines_s],
+        in_specs=[VMEM] * 2,
+        out_specs=[VMEM] * 2,
+        scratch_shapes=[message] * 4 + [block] * 2 + [pltpu.SemaphoreType.DMA((4,))] * 2,
+        compiler_params=pltpu.CompilerParams(
+            vmem_limit_bytes=8 * 2**20, collective_id=0, has_side_effects=True
+        ),
+        name="exchange",
+    )(col_lse, col_lse2)
+    source_pot, target_pot, *_ = pl.pallas_call(
         functools.partial(row_kernel, log_n),
-        out_shape=[lines_s, lines_s, rows_s, cols_s, cols_s, lines_s, u_s],
-        in_specs=[VMEM, SMEM] + [VMEM] * 10,
-        out_specs=[VMEM] * 7,
-        input_output_aliases={11: 2},
+        out_shape=[lines_s, lines_s, rows_s, lines_s, u_s],
+        in_specs=[VMEM, SMEM] + [VMEM] * 7,
+        out_specs=[VMEM] * 5,
+        input_output_aliases={8: 2},
+        scratch_shapes=[pltpu.VMEM((window, 16, cells), BF16)],
         compiler_params=limit,
         name="second_rows",
-    )(at, lists, b, top, k, row_lse, col_lse, right, left, right2, left2, rows)
-
-    total = lse_of([col_lse2[blocks : 2 * blocks], from_right, from_left])
-    target_pot = (0.5 * entropy) * (own_g + log_n - total)
+    )(at, lists, b, top, k, row_lse, g, total, rows)
     return source_pot, target_pot
 
 

time: 318 us -> 306 us (0.962)
  the two profiles are of different devices: /device:TPU:0 before, /device:TPU:120 now
where the time goes in v2:
time: 306 us
  Pallas kernels  300 us (98%)
    pallas_call x1, Pallas kernels, on_device(): pl.pallas_call(functools.partial(far_kernel, log_n), out_shape=[b_s, top_...  139 us
    pallas_call x1, Pallas kernels, on_device(): pl.pallas_call(functools.partial(row_kernel, log_n), out_shape=[lines_s,...  98.2 us
    pallas_call x1, Pallas kernels, on_device(): pl.pallas_call(functools.partial(column_kernel, log_n), out_shape=[cols_s...  40.3 us
    pallas_call x1, Pallas kernels, on_device(): pl.pallas_call(near_kernel, out_shape=[b_s, top_s, k_s, rows_s, cols_s],...  10.9 us
    pallas_call x1, Pallas kernels, on_device(): pl.pallas_call(functools.partial(exchange_kernel, log_n), out_shape=[cols...  7.04 us
  transfers between devices with their start and end apart: 2, of which 0 were waited for; matrix products, arithmetic and copies ran while one was open for 0% of the time, Pallas kernels for 5%

profile of v2, /device:TPU:120, one launch (start us, length us, event | category | flops | bytes accessed | tf_op | source)
XLA Modules:
  0.0 306.2 jit_solution(13180728934076188229)
XLA Ops:
  0.6 0.1 collective-permute-start.1
  0.7 2.7 collective-permute-start
  3.4 5.1 %prepare.1 = (bf16[40,256,64]{2,1,0:T(8,128)(2,1)S(1)}, bf16[121,64,256]{2,1,0:T(8,128)(2,1)S(1)}, s32[784]{0:T(1024)S(4)}, f32[8,256]{1,0:T(8,128)S(1)}) custom-call(bf16[50,40,256]{2,1,0:T(8,128)(2,1)} %bitcast.3, bf16[50,40,256]{2,1,0:T(8,128)(2,1)} %bitcast.6, s32[6,40]{1,0:T(8,128)} %bitcast.7, s32[5120]{0:T(1024)} %home_in.1), custom_call_target="tpu_custom_call" | custom-call | tf_op jit(solution)/shard_map/prepare/pallas_call | solution.py:489
  8.5 0.0 collective-permute-done.1.block_ref
  8.5 0.0 copy-start
  8.5 1.0 copy-done
  9.5 10.9 %near_pairs.1 = (bf16[121,64,256]{2,1,0:T(8,128)(2,1)S(1)}, f32[8,256]{1,0:T(8,128)S(1)}, bf16[243,256,256]{2,1,0:T(8,128)(2,1)S(1)}, f32[40,256,128]{2,1,0:T(8,128)S(1)}, f32[128,256]{1,0:T(8,128)S(1)}) custom-call(bf16[50,40,256]{2,1,0:T(8,128)(2,1)} %copy-done, ...), custom_call_target="tpu_custom_call", output_to_operand_aliasing={{0}: (3, {}), {1}: (4, {})} | custom-call | tf_op jit(solution)/shard_map/near_pairs/pallas_call | solution.py:501
  20.4 0.0 collective-permute-done.block_ref
  20.4 139.1 %far_pairs.1 = (bf16[121,64,256]{2,1,0:T(8,128)(2,1)S(1)}, f32[8,256]{1,0:T(8,128)S(1)}, bf16[243,256,256]{2,1,0:T(8,128)(2,1)S(1)}, f32[40,256,128]{2,1,0:T(8,1...) custom-call(bf16[50,40,256]{2,1,0:T(8,128)(2,1)S(1)} %collective-per, ...), custom_call_target="tpu_custom_call", output_to_operand_aliasing={{0}: (3, {}), {1}: (4, {}), {2}: (5, {}), {3}: (6, {}), {4}... | custom-call | tf_op jit(solution)/shard_map/far_pairs/pallas_call | solution.py:511
  159.4 40.3 %second_columns.1 = (f32[128,256]{1,0:T(8,128)S(1)}, f32[128,256]{1,0:T(8,128)}) custom-call(bf16[40,256,64]{2,1,0:T(8,128)(2,1)S(1)} %get-tuple-element.23.at_ref, s32[784]{0:T(1024)S(4)} %get-tuple-element.24.lists_ref, bf16[121,64,256]{2,1,0:T(8,128)(2,1)S(1)} %get-tuple-element.32.b_ref, f32[8,256]{1,0:T(8,128)S(1)} %get-tuple-element.33.top_ref, ...), custom_call_target="tpu_custom_call" | custom-call | tf_op jit(solution)/shard_map/second_columns/pallas_call | solution.py:522
  199.7 7.0 %exchange.1 = (f32[128,256]{1,0:T(8,128)S(1)}, f32[40,256]{1,0:T(8,128)S(1)}) custom-call(f32[128,256]{1,0:T(8,128)S(1)} %get-tuple-element.36.first_ref, f32[128,256]{1,0:T(8,128)S(1)} %get-tuple-element.39.second_ref), custom_call_target="tpu_custom_call" | custom-call | tf_op jit(solution)/shard_map/exchange/pallas_call | solution.py:532
  206.8 98.2 %second_rows.1 = (f32[40,256]{1,0:T(8,128)S(1)}, f32[40,256]{1,0:T(8,128)S(1)}, f32[40,256,128]{2,1,0:T(8,128)S(1)}, f32[40,256]{1,0:T(8,128)}, bf16[40,256,128]{2,1,0:T(8,128)(2,1)}) custom-call(bf16[40,256,64]{2,1,0:T(8,128)(2,1)S(1)} %get-tuple-element.23.at_ref, s32[784]{0:T(1024)S(4)} %get-tuple-element.24.lists_ref, ...), custom_call_target="tpu_custom_call", output_to_operand_aliasing={{2}: (8, {})} | custom-call | tf_op jit(solution)/shard_map/second_rows/pallas_call | solution.py:543
  304.9 0.6 copy.22
  305.6 0.6 copy.23
Async XLA Ops:
  0.6 7.9 %collective-permute-start.1 = (bf16[50,40,256]{2,1,0:T(8,128)(2,1)}, bf16[50,40,256]{2,1,0:T(8,128)(2,1)S(1)}, u32[]{:S(2)}, u32[]{:S(2)}) collective-permute-start(bf16[50,40,256]{2,1,0:T(8,128)(2,1)} %bitcast.4), channel_id=1, source_target_pairs={{0,1},{1,0},{2,3},{3,2},{4,5},{5,4},{6,7},{7,6},{8,9},{9,8},{10,11... | collective-permute-start | bytes 3072008 | tf_op jit(solution)/shard_map/ppermute | solution.py:473
  0.7 19.6 %collective-permute-start = (bf16[50,40,256]{2,1,0:T(8,128)(2,1)}, bf16[50,40,256]{2,1,0:T(8,128)(2,1)S(1)}, u32[]{:S(2)}, u32[]{:S(2)}) collective-permute-start(bf16[50,40,256]{2,1,0:T(8,128)(2,1)} %bitcast.5), channel_id=1, source_target_pairs={{0,127},{1,2},{2,1},{3,4},{4,3},{5,6},{6,5},{7,8},{8,7},{9,10},{10... | collective-permute-start | bytes 3072008 | tf_op jit(solution)/shard_map/ppermute | solution.py:473
  8.5 1.0 copy-start
